TPU v7x, 32 devices: a whole 2x2x4 slice. The times are simulated.
32 devices in a mesh: dp: 16 (over z, y, x), seq: 2 (over core).
Axes of the slice: x: 2, y: 2, z: 4, core: 2. Of those that a mesh axis runs over, the one named last changes fastest.
Arguments:
- frames: bfloat16 [2, 4096, 768], P(None, ('dp', 'seq')), may hold values from -6 to 6
- clip_lengths: int32 [2, 16, 3], P(None, 'dp'), may hold values from 1 to 192, 256 in all within a row
- conv_weight: bfloat16 [128, 48, 768], P(None, None, 'dp'), may hold values from -0.078125 to 0.078125
- front_gain: bfloat16 [768], P('dp'), may hold values from 0.25 to 1.75
- qkv_weight: bfloat16 [768, 2304], P('dp'), may hold values from -0.3125 to 0.3125
- out_weight: bfloat16 [768, 768], P('dp'), may hold values from -0.875 to 0.875
- middle_gain: bfloat16 [768], P('dp'), may hold values from 0.25 to 1.75
- up_weight: bfloat16 [768, 3072], P('dp'), may hold values from -0.21875 to 0.21875
- down_weight: bfloat16 [3072, 768], P('dp'), may hold values from -0.109375 to 0.109375
- final_gain: bfloat16 [768], P('dp'), may hold values from 0.25 to 1.75
- cotangent: bfloat16 [2, 4096, 768], P(None, ('dp', 'seq')), may hold values from -6 to 6
Outputs:
- output: bfloat16 [2, 4096, 768], P(None, ('dp', 'seq'))
- frames_grad: float32 [2, 4096, 768], P(None, ('dp', 'seq'))
- conv_weight_grad: float32 [128, 48, 768], P(None, None, 'dp')
- front_gain_grad: float32 [768], P('dp')
- qkv_weight_grad: float32 [768, 2304], P('dp')
- out_weight_grad: float32 [768, 768], P('dp')
- middle_gain_grad: float32 [768], P('dp')
- up_weight_grad: float32 [768, 3072], P('dp')
- down_weight_grad: float32 [3072, 768], P('dp')
- final_gain_grad: float32 [768], P('dp')
Inputs may be any that keep to these rules, and one draw needn't show every extreme that they name: `clip_lengths`: the 3 lengths of each pack sum to 256; the longest clip of every pack has exactly 192 frames.
All inputs are finite; a program needn't handle non-finite values.
Results may differ from a plain program's by a relative error of at most 0.019.
Values may be sent and summed in bfloat16 or wider, within the bound.
A program may use at most 176 MiB of HBM per device.

v0:
```python
import functools

import jax
import jax.numpy as jnp
from jax import lax
from jax.experimental import pallas as pl
from jax.experimental.pallas import tpu as pltpu
from jax.sharding import PartitionSpec as P

MESH = pl.DeviceIdType.MESH


def dp_factors(size):
    return {16: (4, 2, 2), 128: (4, 4, 8)}.get(size, (size, 1, 1))


def near_first(size):
    return [1, 3, 2] if size == 4 else list(range(1, size))


def offsets_of(dims):
    return [(i, j, k) for i in range(dims[0]) for j in range(dims[1]) for k in range(dims[2])]


def partner(coordinate, offset):
    bit = 1
    while bit <= offset:
        if offset & bit:
            coordinate = coordinate + bit - 2 * bit * lax.rem(coordinate // bit, 2)
        bit *= 2
    return coordinate


def place(dims, order, position, offsets):
    coords = list(position)
    for axis, offset in zip(order, offsets):
        if offset:
            coords[axis] = partner(coords[axis], offset)
    return (coords[0] * dims[1] + coords[1]) * dims[2] + coords[2]


def position_of(dims):
    me = lax.axis_index("dp")
    return (me // (dims[1] * dims[2]), lax.rem(me // dims[2], dims[1]), lax.rem(me, dims[2]))


def greet(dims, position, core):
    barrier = pltpu.get_barrier_semaphore()
    count = 1
    pl.semaphore_signal(barrier, inc=1, device_id={"seq": 1 - core}, device_id_type=MESH)
    for axis in range(3):
        for offset in range(1, dims[axis]):
            other = place(dims, (axis,), position, (offset,))
            pl.semaphore_signal(barrier, inc=1, device_id={"dp": other}, device_id_type=MESH)
            count += 1
    pl.semaphore_wait(barrier, count)


FIRST = ((0, 1, 2), (0, 2, 1))
SECOND = ((1, 0, 2), (2, 0, 1))
ORDERS = FIRST


def by_core(core_index, body):
    for core in range(2):
        pl.when(core_index == core)(functools.partial(body, core))


class Gather:
    def __init__(self, dims, chunks, ins, outs, sems):
        self.dims, self.chunks, self.ins, self.outs = dims, chunks, ins, outs
        self.send_sems, self.recv_sems, self.push_send, self.push_recv = sems
        self.position = position_of(dims)
        self.count = dims[0] * dims[1] * dims[2]
        self.sent = {}

    def part(self, which, chunk, side):
        source, array, rows, _, lane, lanes = self.chunks[chunk][1 + side]
        out = self.outs[array]
        if len(out.shape) == 3:
            return out.at[which, pl.ds(*rows), pl.ds(lane, lanes)]
        first = pl.multiple_of(which * self.ins[source].shape[0] + rows[0], 16)
        return out.at[pl.ds(first, rows[1]), pl.ds(lane, lanes)]

    def mine(self, chunk, side):
        source, _, rows, lane, _, lanes = self.chunks[chunk][1 + side]
        return self.ins[source].at[pl.ds(*rows), pl.ds(lane, lanes)]

    def own_copies(self, sems):
        me = lax.axis_index("dp")
        return [
            pltpu.make_async_copy(self.mine(chunk, side), self.part(me, chunk, side), sems.at[chunk, side])
            for chunk in range(len(self.chunks))
            for side in range(2)
        ]

    def send(self, core, chunk, offsets, level, distance):
        order = self.chunks[chunk][0][core]
        gid = place(self.dims, order, self.position, offsets)
        number = self.sent.get((core, chunk), 0)
        self.sent[core, chunk] = number + 1
        pltpu.make_async_remote_copy(
            src_ref=self.mine(chunk, core) if offsets == (0, 0, 0) else self.part(gid, chunk, core),
            dst_ref=self.part(gid, chunk, core),
            send_sem=self.send_sems.at[chunk, number],
            recv_sem=self.recv_sems.at[chunk, gid],
            device_id={"dp": place(self.dims, (order[level],), self.position, (distance,))},
            device_id_type=MESH,
        ).start()

    def spread(self, core, chunk, offsets, first):
        for level in range(first, 3):
            for distance in near_first(self.dims[self.chunks[chunk][0][core][level]]):
                self.send(core, chunk, offsets, level, distance)

    def forward(self, core, chunk, offsets, first):
        gid = place(self.dims, self.chunks[chunk][0][core], self.position, offsets)
        ref = self.part(gid, chunk, core)
        pltpu.make_async_copy(ref, ref, self.recv_sems.at[chunk, gid]).wait()
        self.spread(core, chunk, offsets, first)
        pltpu.make_async_remote_copy(
            src_ref=ref,
            dst_ref=ref,
            send_sem=self.push_send.at[chunk, gid],
            recv_sem=self.push_recv.at[chunk, gid],
            device_id={"seq": 1 - core},
            device_id_type=MESH,
        ).start()

    def tasks(self, core, chunk, stage):
        sizes = [self.dims[axis] for axis in self.chunks[chunk][0][core]]
        if stage == 0:
            return [functools.partial(self.spread, core, chunk, (0, 0, 0), 0)]
        if stage == 1:
            places = [(i, 0, 0) for i in near_first(sizes[0])]
        elif stage == 2:
            places = [(i, j, 0) for i in [0] + near_first(sizes[0]) for j in near_first(sizes[1])]
        else:
            places = [
                (i, j, k)
                for j in [0] + near_first(sizes[1])
                for i in [0] + near_first(sizes[0])
                for k in near_first(sizes[2])
            ]
        return [functools.partial(self.forward, core, chunk, offsets, stage) for offsets in places]

    def steps(self, core, step):
        done = []
        for stage in range(4):
            if 0 <= step - stage < len(self.chunks):
                done += self.tasks(core, step - stage, stage)
        return done

    def others(self, body):
        me = lax.axis_index("dp")

        @pl.loop(1, self.count)
        def _(offset):
            body(lax.rem(me + offset, self.count), offset)

    def arrived_block(self, core, chunk, gid):
        ref = self.part(gid, chunk, 1 - core)
        pltpu.make_async_copy(ref, ref, self.push_recv.at[chunk, gid]).wait()

    def arrived(self, core, chunk):
        def body(gid, _):
            ref = self.part(gid, chunk, 1 - core)
            pltpu.make_async_copy(ref, ref, self.push_recv.at[chunk, gid]).wait()

        self.others(body)

    def finish(self, core):
        for chunk in range(len(self.chunks)):

            def body(gid, number, chunk=chunk):
                ref = self.part(gid, chunk, core)
                pltpu.make_async_copy(ref, ref, self.push_send.at[chunk, gid]).wait()
                pltpu.make_async_copy(ref, ref, self.send_sems.at[chunk, number - 1]).wait()

            self.others(body)


def gather_kernel(dims, chunks, *refs):
    n_arr = len(refs[:-5]) // 2
    ins, outs = refs[:n_arr], refs[n_arr : 2 * n_arr]
    gather = Gather(dims, chunks, ins, outs, refs[2 * n_arr : 2 * n_arr + 4])
    local_sems = refs[-1]
    core_index = lax.axis_index("seq")
    greet(dims, gather.position, core_index)
    own = gather.own_copies(local_sems)
    for copy in own:
        copy.start()

    def run(core):
        for step in range(len(chunks) + 3):
            for task in gather.steps(core, step):
                task()
        for chunk in range(len(chunks)):
            gather.arrived(core, chunk)
        gather.finish(core)

    by_core(core_index, run)
    for copy in own:
        copy.wait()


def all_gather(arrays, chunks, dp, collective_id=0):
    dims = dp_factors(dp)
    n = len(chunks)
    any_ = pl.BlockSpec(memory_space=pl.ANY)
    return pl.pallas_call(
        functools.partial(gather_kernel, dims, chunks),
        out_shape=[jax.ShapeDtypeStruct((dp,) + a.shape, a.dtype) for a in arrays],
        in_specs=[any_] * len(arrays),
        out_specs=[any_] * len(arrays),
        scratch_shapes=[
            pltpu.SemaphoreType.DMA((n, dp)),
            pltpu.SemaphoreType.DMA((n, dp)),
            pltpu.SemaphoreType.DMA((n, dp)),
            pltpu.SemaphoreType.DMA((n, dp)),
            pltpu.SemaphoreType.DMA((n, 2)),
        ],
        compiler_params=pltpu.CompilerParams(collective_id=collective_id, has_side_effects=True),
    )(*arrays)


def scatter_kernel(dims, chunks, n_arr, *refs):
    ins, outs = refs[:n_arr], refs[n_arr : 2 * n_arr]
    scratch = list(refs[2 * n_arr :])
    n = len(chunks)
    stage_refs, pair_refs = scratch[:n], scratch[n : 2 * n]
    hop_refs = [scratch[(2 + level) * n : (3 + level) * n] for level in range(3)]
    (load_sems, pair_send, pair_recv, hop_send, hop_recv, last_send, last_recv) = scratch[5 * n :]
    position = position_of(dims)
    core_index = lax.axis_index("seq")
    greet(dims, position, core_index)

    def run(core):
        order = ORDERS[core]
        sizes = [dims[axis] for axis in order]
        started = []
        other_order = ORDERS[1 - core]
        other_sizes = [dims[axis] for axis in other_order]

        def part(array_refs, which, chunk, side):
            array, rows, lanes = chunks[chunk][side]
            return array_refs[array].at[which, pl.ds(*rows), pl.ds(*lanes)]

        def slot(level, offsets, distance):
            index = distance - 1
            for i in range(level):
                index = index * sizes[i] + offsets[i]
            return index

        def semaphore(level, index):
            return (1, sizes[0], sizes[0] * sizes[1])[level] + index - 1

        def begin(chunk):
            array = chunks[chunk][core][0]
            theirs = sorted(offsets_of(other_sizes), key=lambda o: (o[2] == 0, o[1] == 0, o[0] == 0))
            mine = sorted(offsets_of(sizes), key=lambda o: (o[2] == 0, o[1] == 0, o[0] == 0))
            for given, kept in zip(theirs, mine):
                gid = place(dims, other_order, position, given)
                copy = pltpu.make_async_remote_copy(
                    src_ref=part(ins, gid, chunk, 1 - core),
                    dst_ref=pair_refs[chunk].at[gid],
                    send_sem=pair_send.at[chunk],
                    recv_sem=pair_recv.at[chunk, gid],
                    device_id={"seq": 1 - core},
                    device_id_type=MESH,
                )
                copy.start()
                gid = place(dims, order, position, kept)
                pltpu.make_async_copy(
                    part(ins, gid, chunk, core), stage_refs[chunk].at[gid], load_sems.at[chunk, gid]
                ).start()

        def combine(chunk, offsets, target):
            gid = place(dims, order, position, offsets)
            own = stage_refs[chunk].at[gid]
            pair = pair_refs[chunk].at[gid]
            pltpu.make_async_copy(own, own, load_sems.at[chunk, gid]).wait()
            pltpu.make_async_copy(pair, pair, pair_recv.at[chunk, gid]).wait()
            terms = [own, pair]
            for level in (2, 1, 0):
                if offsets[level]:
                    break
                for distance in range(1, sizes[level]):
                    index = slot(level, offsets, distance)
                    ref = hop_refs[level][chunk].at[index]
                    pltpu.make_async_copy(ref, ref, hop_recv.at[chunk, semaphore(level, index)]).wait()
                    terms.append(ref)
            height = own.shape[0]

            tall = 16 if height % 16 == 0 else height

            @pl.loop(0, height // tall)
            def _(tile):
                rows = pl.ds(pl.multiple_of(tile * tall, tall), tall)
                total = terms[0][rows, :].astype(jnp.float32)
                for term in terms[1:]:
                    total = total + term[rows, :].astype(jnp.float32)
                if target is None:
                    own[rows, :] = total.astype(own.dtype)
                else:
                    target[rows, :] = total

            return gid

        def send(chunk, offsets):
            level = max(i for i in range(3) if offsets[i])
            gid = combine(chunk, offsets, None)
            index = slot(level, offsets, offsets[level])
            target = place(dims, (order[level],), position, (offsets[level],))
            copy = pltpu.make_async_remote_copy(
                src_ref=stage_refs[chunk].at[gid],
                dst_ref=hop_refs[level][chunk].at[index],
                send_sem=hop_send.at[chunk, semaphore(level, index)],
                recv_sem=hop_recv.at[chunk, semaphore(level, index)],
                device_id={"dp": target},
                device_id_type=MESH,
            )
            copy.start()
            started.append(copy)

        def final(chunk):
            array, rows, lanes = chunks[chunk][core]
            half = outs[array].at[pl.ds(*rows), pl.ds(*lanes)]
            combine(chunk, (0, 0, 0), half)
            copy = pltpu.make_async_remote_copy(
                src_ref=half,
                dst_ref=half,
                send_sem=last_send.at[chunk],
                recv_sem=last_recv.at[chunk],
                device_id={"seq": 1 - core},
                device_id_type=MESH,
            )
            copy.start()
            started.append(copy)

        for chunk in range(n):
            begin(chunk)

        def stage(chunk, number):
            if number == 0:
                for d in range(1, sizes[2]):
                    for i in range(sizes[0]):
                        for j in range(sizes[1]):
                            send(chunk, (i, (j + 1) % sizes[1], d))
            if number == 1:
                for d in range(1, sizes[1]):
                    for i in range(sizes[0]):
                        send(chunk, ((i + 1) % sizes[0], d, 0))
            if number == 2:
                for d in range(1, sizes[0]):
                    send(chunk, (d, 0, 0))
            if number == 3:
                final(chunk)

        for step in range(n + 3):
            for number in range(4):
                if 0 <= step - number < n:
                    stage(step - number, number)
        for chunk in range(n):
            array, rows, lanes = chunks[chunk][1 - core]
            half = outs[array].at[pl.ds(*rows), pl.ds(*lanes)]
            pltpu.make_async_copy(half, half, last_recv.at[chunk]).wait()
            sent = pair_refs[chunk]
            pltpu.make_async_copy(sent, sent, pair_send.at[chunk]).wait()
        for copy in started:
            copy.wait_send()

    for core in range(2):
        pl.when(core_index == core)(functools.partial(run, core))


def hop_slots(dims, order):
    a, b, c = [dims[axis] for axis in order]
    return (a - 1, a * (b - 1), a * b * (c - 1))


def reduce_scatter(arrays, chunks, dp, collective_id=1):
    dims = dp_factors(dp)
    n = len(chunks)
    any_ = pl.BlockSpec(memory_space=pl.ANY)
    shapes = [(chunk[0][1][1], chunk[0][2][1]) for chunk in chunks]
    slots = [max(pair) for pair in zip(hop_slots(dims, ORDERS[0]), hop_slots(dims, ORDERS[1]))]
    low = jnp.bfloat16
    scratch = [pltpu.VMEM((dp,) + s, low) for s in shapes] * 2
    for level in range(3):
        scratch += [pltpu.VMEM((slots[level],) + s, low) for s in shapes]
    return pl.pallas_call(
        functools.partial(scatter_kernel, dims, chunks, len(arrays)),
        out_shape=[jax.ShapeDtypeStruct(a.shape[1:], jnp.float32) for a in arrays],
        in_specs=[any_] * len(arrays),
        out_specs=[pl.BlockSpec(memory_space=pltpu.VMEM)] * len(arrays),
        scratch_shapes=scratch
        + [
            pltpu.SemaphoreType.DMA((n, dp)),
            pltpu.SemaphoreType.DMA((n,)),
            pltpu.SemaphoreType.DMA((n, dp)),
            pltpu.SemaphoreType.DMA((n, dp)),
            pltpu.SemaphoreType.DMA((n, dp)),
            pltpu.SemaphoreType.DMA((n,)),
            pltpu.SemaphoreType.DMA((n,)),
        ],
        compiler_params=pltpu.CompilerParams(
            collective_id=collective_id, has_side_effects=True, vmem_limit_bytes=58 << 20
        ),
    )(*arrays)


GROUPS = 16
KERNEL = 128
FINE = 16
COARSE = KERNEL // FINE
LANES = 128


def lane_numbers(rows):
    return lax.broadcasted_iota(jnp.int32, (rows, LANES), 1)


def take_group(ref, rows, group, width):
    start = group * width
    base = pl.multiple_of(start // LANES * LANES, LANES)
    window = ref[rows, pl.ds(base, 2 * LANES)]
    turned = pltpu.roll(window, lax.rem(2 * LANES - (start - base), 2 * LANES), 1)[:, :LANES]
    return jnp.where(lane_numbers(turned.shape[0]) < width, turned, 0.0)


def add_group(ref, values, group, width):
    start = group * width
    base = pl.multiple_of(start // LANES * LANES, LANES)
    wide = jnp.concatenate([values, jnp.zeros_like(values)], axis=1)
    ref[:, pl.ds(base, 2 * LANES)] += pltpu.roll(wide, start - base, 1)


def double_96(pair, moved):
    lane = lane_numbers(pair.shape[0])
    turned = pltpu.roll(moved, 96, 1)
    return jnp.where(lane < 96, pair, turned), jnp.where(lane < 64, turned, 0.0)


def double_192(first, second, moved_first, moved_second):
    lane = lane_numbers(first.shape[0])
    a, b = pltpu.roll(moved_first, 64, 1), pltpu.roll(moved_second, 64, 1)
    return first, jnp.where(lane < 64, second, a), jnp.where(lane < 64, a, b)


def fold_lanes(tiles, shift):
    a, b, c = tiles
    lane = lane_numbers(a.shape[0])
    tb, tc = pltpu.roll(b, 64, 1), pltpu.roll(c, 64, 1)
    a, b = shift(a, jnp.where(lane < 64, tb, tc), 4), shift(b, tc, 4)
    lane = lane_numbers(a.shape[0])
    far = jnp.where(lane < 32, pltpu.roll(a, 32, 1), pltpu.roll(b, 32, 1))
    a = shift(a, far, 2)
    a = shift(a, pltpu.roll(a, 80, 1), 1)
    return jnp.where(lane_numbers(a.shape[0]) < 48, a, 0.0)


def make_patch(padded, group, pack):
    reach = pack + FINE
    one = take_group(padded, slice(0, reach + KERNEL - FINE), group, 48)
    rows = one.shape[0] - FINE
    two = one[:rows] + pltpu.roll(one[FINE:], 48, 1)
    low, high = double_96(two[: rows - 2 * FINE], two[2 * FINE :])
    tiles = double_192(low[:reach], high[:reach], low[4 * FINE :], high[4 * FINE :])
    return jnp.concatenate(tiles, axis=1).astype(jnp.bfloat16)


def add_forward(total, patch, weight, group, pack):
    product = jnp.dot(patch, weight, preferred_element_type=jnp.float32)
    size = pack + 8
    near = product[:size, :384] + product[8 : 8 + size, 384:]

    def shift(base, moved, amount):
        return base + pltpu.roll(moved, size - amount, 0)

    tiles = [near[:, i * LANES : (i + 1) * LANES] for i in range(3)]
    add_group(total, fold_lanes(tiles, shift)[:pack], group, 48)


def fill_padded(padded, frames):
    half = KERNEL // 2
    padded[...] = jnp.zeros_like(padded)
    padded[half : half + frames.shape[0], 0 : frames.shape[1]] = frames[...].astype(jnp.float32)


def forward_kernel(pack, frames, weight, out, patches, padded, total):
    group = pl.program_id(0)

    @pl.when(group == 0)
    def _():
        fill_padded(padded, frames)
        total[...] = jnp.zeros_like(total)

    patch = make_patch(padded, group, pack)
    patches[0] = patch
    add_forward(total, patch, weight[0], group, pack)

    @pl.when(group == GROUPS - 1)
    def _():
        out[...] = total[:, : frames.shape[1]]


def conv_forward(frames, weight):
    pack, width = frames.shape
    reach = pack + FINE
    return pl.pallas_call(
        functools.partial(forward_kernel, pack),
        grid=(GROUPS,),
        out_shape=[
            jax.ShapeDtypeStruct((pack, width), jnp.float32),
            jax.ShapeDtypeStruct((GROUPS, reach, 384), jnp.bfloat16),
        ],
        in_specs=[
            pl.BlockSpec((pack, width), lambda g: (0, 0)),
            pl.BlockSpec((1, 384, 768), lambda g: (g, 0, 0)),
        ],
        out_specs=[
            pl.BlockSpec((pack, width), lambda g: (0, 0)),
            pl.BlockSpec((1, reach, 384), lambda g: (g, 0, 0)),
        ],
        scratch_shapes=[
            pltpu.VMEM((pack + KERNEL, width + LANES), jnp.float32),
            pltpu.VMEM((pack, width + LANES), jnp.float32),
        ],
        compiler_params=pltpu.CompilerParams(vmem_limit_bytes=40 << 20),
    )(frames, weight)


def backward_kernel(pack, grads, direct, weight, patches, out, weight_grad, padded, tall, total):
    group = pl.program_id(0)
    reach = pack + FINE
    edge = KERNEL // 2 - FINE

    @pl.when(group == 0)
    def _():
        padded[...] = jnp.zeros_like(padded)
        padded[:pack, : grads.shape[1]] = grads[...].astype(jnp.float32)
        tall[...] = jnp.zeros_like(tall)
        total[...] = jnp.zeros_like(total)
        total[:, : direct.shape[1]] = direct[...]

    def later(values, amount):
        return pltpu.roll(values, amount, 0)

    one = take_group(padded, slice(0, reach), group, 48)
    two = one + pltpu.roll(later(one, 1), 48, 1)
    low, high = double_96(two, later(two, 2))
    tiles = double_192(low, high, later(low, 4), later(high, 4))
    near = jnp.concatenate(tiles, axis=1)
    spread = jnp.concatenate([near, later(near, 8)], axis=1).astype(jnp.bfloat16)
    weight_grad[0] = lax.dot_general(
        patches[0], spread, (((0,), (0,)), ((), ())), preferred_element_type=jnp.float32
    ).astype(jnp.bfloat16)
    tall[edge : edge + reach] = lax.dot_general(
        spread, weight[0], (((1,), (1,)), ((), ())), preferred_element_type=jnp.float32
    )

    def shift(base, moved, amount):
        return base[amount * FINE :] + moved[: base.shape[0] - amount * FINE]

    tiles = [tall[:, i * LANES : (i + 1) * LANES] for i in range(3)]
    add_group(total, fold_lanes(tiles, shift), group, 48)

    @pl.when(group == GROUPS - 1)
    def _():
        out[...] = total[:, : grads.shape[1]]


def conv_backward(grads, direct, weight, patches):
    pack, width = grads.shape
    reach = pack + FINE
    whole = lambda g: (0, 0)
    each = lambda g: (g, 0, 0)
    return pl.pallas_call(
        functools.partial(backward_kernel, pack),
        grid=(GROUPS,),
        out_shape=[
            jax.ShapeDtypeStruct((pack, width), jnp.float32),
            jax.ShapeDtypeStruct(weight.shape, jnp.bfloat16),
        ],
        in_specs=[
            pl.BlockSpec((pack, width), whole),
            pl.BlockSpec((pack, width), whole),
            pl.BlockSpec((1, 384, 768), each),
            pl.BlockSpec((1, reach, 384), each),
        ],
        out_specs=[
            pl.BlockSpec((pack, width), whole),
            pl.BlockSpec((1, 384, 768), each),
        ],
        scratch_shapes=[
            pltpu.VMEM((reach, width + LANES), jnp.float32),
            pltpu.VMEM((pack + KERNEL - FINE, 384), jnp.float32),
            pltpu.VMEM((pack, width + LANES), jnp.float32),
        ],
        compiler_params=pltpu.CompilerParams(vmem_limit_bytes=40 << 20),
    )(grads, direct, weight, patches)


HEAD_DIM = 64
EPSILON = 1e-05
ROWS = 32
TILE = 256


def dot(a, b, contract=(1, 0)):
    return lax.dot_general(
        a, b, ((contract[:1], contract[1:]), ((), ())), preferred_element_type=jnp.float32
    )


def below_normal(values):
    return 0.5 * (1.0 + lax.erf(values * 0.7071067811865476))


def density(values):
    return jnp.exp(-0.5 * values * values) * 0.3989422804014327


def unit_norm(values):
    centered = values - jnp.mean(values, axis=-1, keepdims=True)
    inverse = lax.rsqrt(jnp.mean(centered * centered, axis=-1, keepdims=True) + EPSILON)
    return centered * inverse, inverse


def norm_back(grad, unit, inverse, gain):
    scaled = grad * gain
    inner = jnp.mean(scaled, axis=-1, keepdims=True)
    along = jnp.mean(scaled * unit, axis=-1, keepdims=True)
    return inverse * (scaled - inner - unit * along)


def row_tiles(pack, body):
    @pl.loop(0, pack // ROWS)
    def _(tile):
        body(pl.ds(pl.multiple_of(tile * ROWS, ROWS), ROWS))


def lane_tiles(count, body, first=0):
    @pl.loop(first, count)
    def _(tile):
        body(tile, pl.ds(pl.multiple_of(tile * TILE, TILE), TILE))


def clip_mask(lengths, micro, pack):
    row = lax.broadcasted_iota(jnp.int32, (pack, pack), 0)
    column = lax.broadcasted_iota(jnp.int32, (pack, pack), 1)
    row_clip, column_clip = jnp.zeros_like(row), jnp.zeros_like(column)
    end = 0
    for clip in range(lengths.shape[1]):
        end = end + lengths[micro, clip]
        row_clip += (row >= end).astype(jnp.int32)
        column_clip += (column >= end).astype(jnp.int32)
    return row_clip == column_clip


def front_norm(frames, convolved, gains, normed, normed_low, unit, inverse, front_slope):
    def body(rows):
        values = convolved[rows, 0 : frames.shape[1]]
        below = below_normal(values)
        front_slope[rows, :] = below + values * density(values)
        mixed = frames[rows, :].astype(jnp.float32) + values * below
        units, inv = unit_norm(mixed)
        unit[rows, :] = units
        inverse[rows, :] = jnp.broadcast_to(inv, (ROWS, LANES))
        total = units * gains[0:1, :]
        normed[rows, :] = total
        normed_low[rows, :] = total.astype(normed_low.dtype)

    row_tiles(frames.shape[0], body)


def project(normed_low, weight, projected):
    def body(tile, lanes):
        projected[:, lanes] = dot(normed_low[...], weight[:, lanes]).astype(projected.dtype)

    lane_tiles(projected.shape[1] // TILE, body)


def pair_parts(projected, pair, width):
    return [
        projected[:, pl.ds(pl.multiple_of(part * width + pair * LANES, LANES), LANES)] for part in range(3)
    ]


def attend(projected, lengths, micro, probs, attended, first=0, last=None):
    pack, width = attended.shape
    low = projected.dtype
    scale = HEAD_DIM ** (-0.5)

    @pl.loop(first, last or width // LANES)
    def _(pair):
        same = clip_mask(lengths, micro, pack)
        queries, keys, values = pair_parts(projected, pair, width)
        lane = lax.broadcasted_iota(jnp.int32, (pack, LANES), 1)
        sides = []
        for side in range(2):
            own = (lane < HEAD_DIM) == (side == 0)
            scores = dot(jnp.where(own, queries, jnp.zeros_like(queries)), keys, (1, 1)) * scale
            scores = jnp.where(same, scores, -1e30)
            shifted = jnp.exp(scores - jnp.max(scores, axis=-1, keepdims=True))
            weights = shifted / jnp.sum(shifted, axis=-1, keepdims=True)
            probs[2 * pair + side] = weights
            sides.append(dot(weights.astype(low), values))
        lanes = pl.ds(pl.multiple_of(pair * LANES, LANES), LANES)
        attended[:, lanes] = jnp.where(lane < HEAD_DIM, *sides).astype(low)


def middle_norm(attended, weight, normed, gains, middle, middle_low, unit, inverse):
    def body(tile, lanes):
        middle[:, lanes] = normed[:, lanes] + dot(attended[...], weight[:, lanes])

    lane_tiles(normed.shape[1] // TILE, body)

    def finish(rows):
        units, inv = unit_norm(middle[rows, :])
        unit[rows, :] = units
        inverse[rows, :] = jnp.broadcast_to(inv, (ROWS, LANES))
        total = units * gains[1:2, :]
        middle[rows, :] = total
        middle_low[rows, :] = total.astype(middle_low.dtype)

    row_tiles(normed.shape[0], finish)


def feed_up(middle_low, weight, slope, activated, first=0, last=None):
    def body(tile, lanes):
        values = dot(middle_low[...], weight[:, lanes])
        below = below_normal(values)
        slope[:, lanes] = (below + values * density(values)).astype(slope.dtype)
        activated[:, lanes] = (values * below).astype(activated.dtype)

    lane_tiles(last or slope.shape[1] // TILE, body, first)


def feed_down(activated, weight, middle, gains, cotangent, output, grad_final, gain_grads):
    def body(tile, lanes):
        middle[...] += dot(activated[:, lanes], weight[lanes, :])

    lane_tiles(activated.shape[1] // TILE, body)
    gain_grads[2:3, :] = jnp.zeros((1, middle.shape[1]), jnp.float32)

    def finish(rows):
        units, inv = unit_norm(middle[rows, :])
        gain = gains[2:3, :]
        output[rows, :] = (units * gain).astype(output.dtype)
        grad = cotangent[rows, :].astype(jnp.float32)
        gain_grads[2:3, :] += jnp.sum(grad * units, axis=0, keepdims=True)
        grad_final[rows, :] = norm_back(grad, units, inv, gain)

    row_tiles(middle.shape[0], finish)


def feed_back(grad, slope, activated, middle_low, up, down, up_grad, down_grad):
    low = activated.dtype
    grad_feed = grad[...].astype(low)
    turned = jnp.transpose(middle_low[...].astype(jnp.float32)).astype(low)

    def body(tile, lanes):
        down_grad[lanes, :] = dot(activated[:, lanes], grad_feed, (0, 0)).astype(low)
        grad_hidden = (dot(grad_feed, down[lanes, :], (1, 1)) * slope[:, lanes].astype(jnp.float32)).astype(low)
        up_grad[:, lanes] = dot(turned, grad_hidden).astype(low)
        grad[...] += dot(grad_hidden, up[:, lanes], (1, 1))

    lane_tiles(slope.shape[1] // TILE, body)


def norm_back_rows(grad, unit, inverse, gains, which, gain_grads):
    gain_grads[which : which + 1, :] = jnp.zeros((1, grad.shape[1]), jnp.float32)

    def body(rows):
        incoming, units = grad[rows, :], unit[rows, :]
        gain_grads[which : which + 1, :] += jnp.sum(incoming * units, axis=0, keepdims=True)
        grad[rows, :] = norm_back(incoming, units, inverse[rows, 0:1], gains[which : which + 1, :])

    row_tiles(grad.shape[0], body)


def branch_back(grad, attended, weight, grad_attended, out_grad):
    low = attended.dtype
    grad_branch = grad[...].astype(low)

    def body(tile, lanes):
        out_grad[lanes, :] = dot(attended[:, lanes], grad_branch, (0, 0)).astype(low)
        grad_attended[:, lanes] = dot(grad_branch, weight[lanes, :], (1, 1)).astype(low)

    lane_tiles(attended.shape[1] // TILE, body)


def attend_back_pair(projected, grad_attended, weights_of, grad_projected, pair):
    pack, width = grad_attended.shape
    low = projected.dtype
    scale = HEAD_DIM ** (-0.5)

    def lanes_of(part):
        start = part * width + pair * LANES
        return pl.ds(start if isinstance(pair, int) else pl.multiple_of(start, LANES), LANES)

    queries, keys, values = [projected[:, lanes_of(part)] for part in range(3)]
    grad = grad_attended[:, lanes_of(0)]
    lane = lax.broadcasted_iota(jnp.int32, (pack, LANES), 1)
    sides = []
    for side in range(2):
        own = (lane < HEAD_DIM) == (side == 0)
        weights = weights_of[side]
        grad_values = dot(weights.astype(low), grad, (0, 0))
        grad_probs = dot(jnp.where(own, grad, jnp.zeros_like(grad)), values, (1, 1))
        along = jnp.sum(weights * grad_probs, axis=-1, keepdims=True)
        grad_scores = (weights * (grad_probs - along)).astype(low)
        grad_queries = dot(grad_scores, keys) * scale
        grad_keys = dot(grad_scores, queries, (0, 0)) * scale
        sides.append((grad_queries, grad_keys, grad_values))
    for part in range(3):
        grad_projected[:, lanes_of(part)] = jnp.where(lane < HEAD_DIM, sides[0][part], sides[1][part]).astype(low)


def attend_back(projected, grad_attended, probs, grad_projected):
    @pl.loop(0, grad_attended.shape[1] // LANES)
    def _(pair):
        attend_back_pair(projected, grad_attended, probs.at[pl.ds(2 * pair, 2)], grad_projected, pair)


def project_back(grad, grad_projected, unit, gains, weight, qkv_grad):
    low = grad_projected.dtype
    turned = jnp.transpose(unit[...] * gains[0:1, :]).astype(low)

    def body(tile, lanes):
        qkv_grad[:, lanes] = dot(turned, grad_projected[:, lanes]).astype(low)
        grad[...] += dot(grad_projected[:, lanes], weight[:, lanes], (1, 1))

    lane_tiles(grad_projected.shape[1] // TILE, body)


def slope_rows(grad, front_slope, grad_convolved):
    def body(rows):
        grad_convolved[rows, :] = (grad[rows, :] * front_slope[rows, :]).astype(grad_convolved.dtype)

    row_tiles(grad.shape[0], body)


def middle_forward_kernel(
    lengths, frames, convolved, gains, wide, down, cotangent,
    output, front_slope, grad_final, unit_front, inverse_front, projected, probs, attended,
    unit_middle, inverse_middle, middle_low, slope, activated, gain_grads,
    normed, normed_low, middle,
):
    width = frames.shape[1]
    gain_grads[...] = jnp.zeros_like(gain_grads)
    front_norm(frames, convolved, gains, normed, normed_low, unit_front, inverse_front, front_slope)
    project(normed_low, wide.at[:, 0 : 3 * width], projected)
    attend(projected, lengths, 0, probs, attended)
    middle_norm(
        attended, wide.at[:, 3 * width : 4 * width], normed, gains, middle, middle_low, unit_middle,
        inverse_middle,
    )
    feed_up(middle_low, wide.at[:, 4 * width :], slope, activated)
    feed_down(activated, down, middle, gains, cotangent, output, grad_final, gain_grads)


def middle_backward_kernel(
    gains, wide, down, front_slope, grad_final, unit_front, inverse_front, projected, probs, attended,
    unit_middle, inverse_middle, middle_low, slope, activated, last_gain_grad,
    grad, grad_convolved, wide_grad, down_grad, gain_grads,
    grad_attended, grad_projected,
):
    width = grad.shape[1]
    gain_grads[...] = last_gain_grad[...]
    grad[...] = grad_final[...]
    feed_back(
        grad, slope, activated, middle_low, wide.at[:, 4 * width :], down, wide_grad.at[:, 4 * width :],
        down_grad,
    )
    norm_back_rows(grad, unit_middle, inverse_middle, gains, 1, gain_grads)
    branch_back(
        grad, attended, wide.at[:, 3 * width : 4 * width], grad_attended,
        wide_grad.at[:, 3 * width : 4 * width],
    )
    attend_back(projected, grad_attended, probs, grad_projected)
    project_back(
        grad, grad_projected, unit_front, gains, wide.at[:, 0 : 3 * width], wide_grad.at[:, 0 : 3 * width]
    )
    norm_back_rows(grad, unit_front, inverse_front, gains, 0, gain_grads)
    slope_rows(grad, front_slope, grad_convolved)


def middle_forward(frames, convolved, lengths, gains, wide, down, cotangent):
    pack, width = frames.shape
    inner = down.shape[0]
    heads = width // HEAD_DIM
    low, full = jnp.bfloat16, jnp.float32
    shape = jax.ShapeDtypeStruct
    vmem = pl.BlockSpec(memory_space=pltpu.VMEM)
    saved = [
        shape((pack, width), low),
        shape((pack, width), full),
        shape((pack, width), full),
        shape((pack, width), full),
        shape((pack, LANES), full),
        shape((pack, 3 * width), low),
        shape((heads, pack, pack), full),
        shape((pack, width), low),
        shape((pack, width), full),
        shape((pack, LANES), full),
        shape((pack, width), low),
        shape((pack, inner), low),
        shape((pack, inner), low),
        shape((8, width), full),
    ]
    return pl.pallas_call(
        middle_forward_kernel,
        out_shape=saved,
        in_specs=[pl.BlockSpec(memory_space=pltpu.SMEM)] + [vmem] * 6,
        out_specs=[vmem] * len(saved),
        scratch_shapes=[
            pltpu.VMEM((pack, width), full),
            pltpu.VMEM((pack, width), low),
            pltpu.VMEM((pack, width), full),
        ],
        compiler_params=pltpu.CompilerParams(vmem_limit_bytes=58 << 20),
    )(lengths, frames, convolved, gains, wide, down, cotangent)


def middle_backward(gains, wide, down, kept):
    pack, width = kept[0].shape
    low, full = jnp.bfloat16, jnp.float32
    shape = jax.ShapeDtypeStruct
    vmem = pl.BlockSpec(memory_space=pltpu.VMEM)
    grads = [
        shape((pack, width), full),
        shape((pack, width), low),
        shape(wide.shape, low),
        shape(down.shape, low),
        shape((8, width), full),
    ]
    return pl.pallas_call(
        middle_backward_kernel,
        out_shape=grads,
        in_specs=[vmem] * (3 + len(kept)),
        out_specs=[vmem] * len(grads),
        scratch_shapes=[pltpu.VMEM((pack, width), low), pltpu.VMEM((pack, 3 * width), low)],
        compiler_params=pltpu.CompilerParams(vmem_limit_bytes=58 << 20),
    )(gains, wide, down, *kept)


def weave(tasks, pieces):
    core_index = lax.axis_index("seq")
    count, done = len(tasks[0]), 0
    for number, piece in enumerate(pieces + [None]):
        until = count if piece is None else (number + 1) * count // (len(pieces) + 1)

        def some(core, first=done, last=until):
            for task in tasks[core][first:last]:
                task()

        if until > done:
            by_core(core_index, some)
        done = until
        if piece is not None:
            piece()


def fused_forward_kernel(
    dims, chunks,
    lengths, frames, cotangent, conv_shard, qkv_shard, out_shard, up_shard, down_shard, front_gain, middle_gain,
    final_gain,
    conv_out, wide_out, down_out, patches_out, front_slope_out, unit_front_out, projected_out, probs_out,
    attended_out, unit_middle_out, middle_low_out, both_output, gains, grad_final, inverse_front, inverse_middle,
    slope, activated, gain_grads,
    patches, front_slope, unit_front, projected, probs, attended, unit_middle, middle_low, gain_shard,
    conv_all, wide_all, down_all, gain_all, pack_frames, pack_cotangent, output, padded, total,
    gains_wide, normed, normed_low, middle,
    send_sems, recv_sems, push_send, push_recv, own_sems, local_sems, save_sems, pair_sems,
):
    ins = (conv_shard, qkv_shard, out_shard, up_shard, down_shard, gain_shard)
    outs = (conv_all, wide_all, down_all, gain_all)
    gather = Gather(dims, chunks, ins, outs, (send_sems, recv_sems, push_send, push_recv))
    core_index = lax.axis_index("seq")
    pack, width = pack_frames.shape
    half = pack // 2
    row = lax.broadcasted_iota(jnp.int32, (GAIN_ROWS, LANES), 0)
    rows = jnp.zeros((GAIN_ROWS, LANES), jnp.float32)
    for index, gain in enumerate((front_gain, middle_gain, final_gain)):
        one = gain[...].astype(jnp.float32)
        one = jnp.concatenate([one, jnp.zeros((1, LANES - one.shape[1]), jnp.float32)], axis=1)
        rows = jnp.where(row == index, one, rows)
    gain_shard[...] = jnp.concatenate([rows, rows], axis=0).astype(gain_shard.dtype)
    greet(dims, gather.position, core_index)

    here = pl.ds(pl.multiple_of(core_index * half, half), half)
    there = pl.ds(pl.multiple_of((1 - core_index) * half, half), half)

    def to_partner(source, target, number):
        return pltpu.make_async_remote_copy(
            src_ref=source,
            dst_ref=target,
            send_sem=pair_sems.at[0, number],
            recv_sem=pair_sems.at[1, number],
            device_id={"seq": 1 - core_index},
            device_id_type=MESH,
        )

    moves = []
    for number, (source, target) in enumerate(((frames, pack_frames), (cotangent, pack_cotangent))):
        moves.append(to_partner(source.at[1 - core_index], target.at[here], number))
        moves.append(pltpu.make_async_copy(source.at[core_index], target.at[here], local_sems.at[number]))
    for copy in moves:
        copy.start()
    own = gather.own_copies(own_sems)
    for copy in own:
        copy.start()

    def early(core):
        for chunk in range(3):
            for task in gather.tasks(core, chunk, 0):
                task()

    by_core(core_index, early)
    steps = []
    for step in range(1, len(chunks) + 3):
        both = []
        for core in range(2):
            tasks = []
            if 3 <= step + 2 < len(chunks):
                tasks += gather.tasks(core, step + 2, 0)
            for stage in (1, 2, 3):
                if 0 <= step - stage < len(chunks):
                    tasks += gather.tasks(core, step - stage, stage)
            both.append(tasks)
        steps.append(both)

    def gate(*numbers):
        def body(core):
            for number in numbers:
                gather.arrived(core, number)

        by_core(core_index, body)

    for copy in moves[:2]:
        copy.wait()
    fill_padded(padded, pack_frames)
    total[...] = jnp.zeros_like(total)

    def patch_piece(first, last):
        def piece():
            @pl.loop(first, last)
            def _(group):
                patches[group] = make_patch(padded, group, pack)

        return piece

    rank = [0] + near_first(dims[0])
    places = sorted(offsets_of(dims), key=lambda o: ((o[1] != 0) + (o[2] != 0), rank.index(o[0])))

    def conv_piece(offsets):
        group = place(dims, (0, 1, 2), gather.position, offsets)

        def wait(core):
            for chunk in (1, 2):
                gather.arrived_block(core, chunk, group)

        def piece():
            if offsets != (0, 0, 0):
                by_core(core_index, wait)
            add_forward(total, patches[group], conv_all[group], group, pack)

        return piece

    quarter = GROUPS // 4
    early_pieces = [patch_piece(i * quarter, (i + 1) * quarter) for i in range(4)]
    weave(steps[0], early_pieces[:1])
    weave(steps[1], early_pieces[1:3])
    weave(steps[2], early_pieces[3:])
    for copy in own:
        copy.wait()
    conv_pieces = [conv_piece(offsets) for offsets in places]
    alone = sum(1 for offsets in places if not (offsets[1] or offsets[2]))
    pairs = sum(1 for offsets in places if offsets[1] and offsets[2])
    weave(steps[3], conv_pieces[:alone])
    last = len(gather.tasks(0, 2, 3))
    weave([tasks[:-last] for tasks in steps[4]], [])
    taken = alone
    for number in range(last):
        many = 1 if number >= last - pairs else (len(places) - alone - pairs) // (last - pairs)
        weave([tasks[number - last :][:1] for tasks in steps[4]], [])
        for piece in conv_pieces[taken : taken + many]:
            piece()
        taken += many
    gate(0)
    saves = []

    def save(source, target):
        copy = pltpu.make_async_copy(source, target, save_sems.at[len(saves)])
        copy.start()
        saves.append(copy)

    save(patches, patches_out)
    save(conv_all, conv_out)
    gains_wide[...] = jnp.zeros_like(gains_wide)

    @pl.loop(0, gather.count)
    def _(shard):
        add_group(gains_wide, gain_all[shard, 0:16, :].astype(jnp.float32), shard, width // gather.count)

    gains[...] = gains_wide[0:8, 0:width]
    def front_piece():
        front_norm(pack_frames, total, gains, normed, normed_low, unit_front, inverse_front, front_slope)
        save(front_slope, front_slope_out)
        save(unit_front, unit_front_out)

    def project_piece():
        gate(3)
        project(normed_low, wide_all.at[:, 0 : 3 * width], projected)
        save(projected, projected_out)

    def attend_piece(first, last):
        return lambda: attend(projected, lengths, core_index, probs, attended, first, last)

    def middle_piece():
        gate(4)
        save(probs, probs_out)
        save(attended, attended_out)
        middle_norm(
            attended, wide_all.at[:, 3 * width : 4 * width], normed, gains, middle, middle_low, unit_middle,
            inverse_middle,
        )
        save(unit_middle, unit_middle_out)
        save(middle_low, middle_low_out)

    head_pairs = width // LANES
    weave(steps[5], [front_piece])
    weave(steps[6], [project_piece] + [attend_piece(i, i + 2) for i in range(0, head_pairs, 2)])
    weave(steps[7], [middle_piece])
    up = wide_all.at[:, 4 * width :]
    count = slope.shape[1] // TILE
    third = count // 3

    def up_piece(first):
        def piece():
            if first == 0:
                gate(5)
                save(wide_all, wide_out)
            feed_up(middle_low, up, slope, activated, first, first + third)

        return piece

    weave(steps[8], [up_piece(i) for i in range(0, count, third)])
    gate(6)
    save(down_all, down_out)
    for copy in moves[2:]:
        copy.wait()
    gain_grads[...] = jnp.zeros_like(gain_grads)
    feed_down(activated, down_all, middle, gains, pack_cotangent, output, grad_final, gain_grads)
    last = to_partner(output.at[there], both_output.at[core_index], 2)
    last.start()
    stay = pltpu.make_async_copy(output.at[here], both_output.at[core_index], local_sems.at[2])
    stay.start()
    by_core(core_index, gather.finish)
    for copy in saves + [stay, last]:
        copy.wait()


def fused_forward(frames, cotangent, lengths, shards_in, chunks, dp):
    dims = dp_factors(dp)
    n = len(chunks)
    conv_shard, qkv_shard, out_shard, up_shard, down_shard = shards_in[:5]
    pack, width = 2 * frames.shape[1], frames.shape[2]
    inner = down_shard.shape[0] * dp
    heads = width // HEAD_DIM
    low, full = jnp.bfloat16, jnp.float32
    shape = jax.ShapeDtypeStruct
    vmem = pl.BlockSpec(memory_space=pltpu.VMEM)
    any_ = pl.BlockSpec(memory_space=pl.ANY)
    conv_shape = (dp,) + conv_shard.shape
    wide_shape = (width, 4 * width + up_shard.shape[1])
    down_shape = (inner, width)
    kept = [
        shape((GROUPS, pack + FINE, 384), low),
        shape((pack, width), full),
        shape((pack, width), full),
        shape((pack, 3 * width), low),
        shape((heads, pack, pack), full),
        shape((pack, width), low),
        shape((pack, width), full),
        shape((pack, width), low),
    ]
    saved = [
        shape(frames.shape, low),
        shape((8, width), full),
        shape((pack, width), full),
        shape((pack, LANES), full),
        shape((pack, LANES), full),
        shape((pack, inner), low),
        shape((pack, inner), low),
        shape((8, width), full),
    ]
    return pl.pallas_call(
        functools.partial(fused_forward_kernel, dims, chunks),
        out_shape=[shape(conv_shape, low), shape(wide_shape, low), shape(down_shape, low)] + kept + saved,
        in_specs=[pl.BlockSpec(memory_space=pltpu.SMEM)] + [any_] * 7 + [vmem] * 3,
        out_specs=[any_] * 11 + [vmem] * len(saved),
        scratch_shapes=[pltpu.VMEM(one.shape, one.dtype) for one in kept]
        + [
            pltpu.VMEM((2 * GAIN_ROWS, LANES), low),
            pltpu.VMEM(conv_shape, low),
            pltpu.VMEM(wide_shape, low),
            pltpu.VMEM(down_shape, low),
            pltpu.VMEM((dp, 2 * GAIN_ROWS, LANES), low),
            pltpu.VMEM((pack, width), low),
            pltpu.VMEM((pack, width), low),
            pltpu.VMEM((pack, width), low),
            pltpu.VMEM((pack + KERNEL, width + LANES), full),
            pltpu.VMEM((pack, width + LANES), full),
            pltpu.VMEM((16, width + LANES), full),
            pltpu.VMEM((pack, width), full),
            pltpu.VMEM((pack, width), low),
            pltpu.VMEM((pack, width), full),
            pltpu.SemaphoreType.DMA((n, dp)),
            pltpu.SemaphoreType.DMA((n, dp)),
            pltpu.SemaphoreType.DMA((n, dp)),
            pltpu.SemaphoreType.DMA((n, dp)),
            pltpu.SemaphoreType.DMA((n, 2)),
            pltpu.SemaphoreType.DMA((3,)),
            pltpu.SemaphoreType.DMA((11,)),
            pltpu.SemaphoreType.DMA((2, 3)),
        ],
        compiler_params=pltpu.CompilerParams(
            collective_id=2, has_side_effects=True, vmem_limit_bytes=60 << 20
        ),
    )(lengths, frames, cotangent, *shards_in)


STRIP = 384
DOWN, UP, OUT, QKV, GAIN, CONV = range(6)
CONV_PARTS = 4
SCATTER_ORDERS = (FIRST, FIRST, FIRST, FIRST, FIRST) + (FIRST,) * CONV_PARTS


class Scatter:
    def __init__(self, dims, heights, stages, pairs, hops, outs, conv_pair, sems):
        self.dims, self.heights = dims, heights
        self.stages, self.pairs, self.hops, self.outs, self.conv_pair = stages, pairs, hops, outs, conv_pair
        self.waited = set()
        self.pair_recv, self.hop_send, self.hop_recv, self.last_send, self.last_recv = sems
        self.position = position_of(dims)
        self.count = dims[0] * dims[1] * dims[2]

    def block(self, ref, chunk, gid):
        if len(ref.shape) == 3:
            return ref.at[gid]
        height = self.heights[chunk]
        return ref.at[pl.ds(pl.multiple_of(gid * height, 16), height)]

    def sizes(self, core, chunk):
        return [self.dims[axis] for axis in SCATTER_ORDERS[chunk][core]]

    def slot(self, core, chunk, level, offsets, distance):
        index = distance - 1
        for i in range(level):
            index = index * self.sizes(core, chunk)[i] + offsets[i]
        return index

    def semaphore(self, core, chunk, level, index):
        sizes = self.sizes(core, chunk)
        return (1, sizes[0], sizes[0] * sizes[1])[level] + index - 1

    def combine(self, core, chunk, offsets, target):
        order = SCATTER_ORDERS[chunk][core]
        gid = place(self.dims, order, self.position, offsets)
        own, pair = self.block(self.stages[chunk], chunk, gid), self.block(self.pairs[chunk], chunk, gid)
        natural = (core,) + tuple(offset for _, offset in sorted(zip(order, offsets)))
        if chunk >= CONV and natural not in self.waited:
            self.waited.add(natural)
            whole = self.conv_pair.at[gid]
            pltpu.make_async_copy(whole, whole, self.pair_recv.at[CONV, gid]).wait()
        terms = [own, pair]
        for level in (2, 1, 0):
            if offsets[level]:
                break
            for distance in range(1, self.sizes(core, chunk)[level]):
                index = self.slot(core, chunk, level, offsets, distance)
                ref = self.hops[level][chunk].at[index]
                number = self.semaphore(core, chunk, level, index)
                pltpu.make_async_copy(ref, ref, self.hop_recv.at[chunk, number]).wait()
                terms.append(ref)

        tall = 48 if own.shape[0] % 48 == 0 else 16

        @pl.loop(0, own.shape[0] // tall)
        def _(tile):
            rows = pl.ds(pl.multiple_of(tile * tall, 16), tall)
            if target is None and len(terms) == 2:
                own[rows, :] = own[rows, :] + pair[rows, :]
                return
            total = terms[0][rows, :].astype(jnp.float32)
            for term in terms[1:]:
                total = total + term[rows, :].astype(jnp.float32)
            if target is None:
                own[rows, :] = total.astype(own.dtype)
            else:
                target[rows, :] = total

        return own

    def send(self, core, chunk, offsets):
        level = max(i for i in range(3) if offsets[i])
        own = self.combine(core, chunk, offsets, None)
        index = self.slot(core, chunk, level, offsets, offsets[level])
        number = self.semaphore(core, chunk, level, index)
        pltpu.make_async_remote_copy(
            src_ref=own,
            dst_ref=self.hops[level][chunk].at[index],
            send_sem=self.hop_send.at[chunk, number],
            recv_sem=self.hop_recv.at[chunk, number],
            device_id={"dp": place(self.dims, (SCATTER_ORDERS[chunk][core][level],), self.position, (offsets[level],))},
            device_id_type=MESH,
        ).start()

    def half(self, chunk, core):
        out = self.outs[chunk]
        lanes = out.shape[1] // 2
        return out.at[:, pl.ds(core * lanes, lanes)]

    def final(self, core, chunk):
        half = self.half(chunk, core)
        self.combine(core, chunk, (0, 0, 0), half)
        pltpu.make_async_remote_copy(
            src_ref=half,
            dst_ref=half,
            send_sem=self.last_send.at[chunk],
            recv_sem=self.last_recv.at[chunk],
            device_id={"seq": 1 - core},
            device_id_type=MESH,
        ).start()

    def tasks(self, core, chunk, stage):
        sizes = self.sizes(core, chunk)
        if stage == 3:
            return [functools.partial(self.final, core, chunk)]
        if stage == 2:
            places = [(i, 0, 0) for i in near_first(sizes[0])[::-1]]
        elif stage == 1:
            places = [(i, d, 0) for d in near_first(sizes[1]) for i in near_first(sizes[0])[::-1] + [0]]
        else:
            places = [
                (i, j, d)
                for d in near_first(sizes[2])
                for j in near_first(sizes[1]) + [0]
                for i in near_first(sizes[0])[::-1] + [0]
            ]
        return [functools.partial(self.send, core, chunk, offsets) for offsets in places]

    def finish(self, core):
        for chunk in range(len(self.outs)):
            half = self.half(chunk, 1 - core)
            pltpu.make_async_copy(half, half, self.last_recv.at[chunk]).wait()
            pltpu.make_async_copy(half, half, self.last_send.at[chunk]).wait()

            @pl.loop(0, self.count - 1)
            def _(number, chunk=chunk):
                ref = self.block(self.stages[chunk], chunk, 0)
                pltpu.make_async_copy(ref, ref, self.hop_send.at[chunk, number]).wait()


class Stream:
    def __init__(self, buffer, sems):
        self.buffer, self.sems = buffer, sems

    def start(self, source, number):
        pltpu.make_async_copy(source, self.buffer.at[number % 2], self.sems.at[number % 2]).start()

    def take(self, number):
        ref = self.buffer.at[number % 2]
        pltpu.make_async_copy(ref, ref, self.sems.at[number % 2]).wait()
        return ref


class Outbox:
    def __init__(self, buffer, sems):
        self.buffer, self.sems, self.busy, self.number = buffer, sems, [None, None], 0

    def free(self):
        slot = self.number % 2
        self.number += 1
        if self.busy[slot] is not None:
            self.busy[slot].wait_send()
            self.busy[slot] = None
        return slot, self.buffer.at[slot]

    def send(self, slot, source, target, recv_sem):
        copy = pltpu.make_async_remote_copy(
            src_ref=source,
            dst_ref=target,
            send_sem=self.sems.at[slot],
            recv_sem=recv_sem,
            device_id={"seq": 1 - lax.axis_index("seq")},
            device_id_type=MESH,
        )
        copy.start()
        self.busy[slot] = copy

    def drain(self):
        for copy in self.busy:
            if copy is not None:
                copy.wait_send()
        self.busy = [None, None]


def spread_grads(padded, group, pack):
    def later(values, amount):
        return pltpu.roll(values, amount, 0)

    one = take_group(padded, slice(0, pack + FINE), group, 48)
    two = one + pltpu.roll(later(one, 1), 48, 1)
    low, high = double_96(two, later(two, 2))
    near = jnp.concatenate(double_192(low, high, later(low, 4), later(high, 4)), axis=1)
    return jnp.concatenate([near, later(near, 8)], axis=1).astype(jnp.bfloat16)


def add_backward(total, tall, spread, weight, group, pack):
    edge = KERNEL // 2 - FINE
    tall[edge : edge + pack + FINE] = dot(spread, weight, (1, 1))

    def shift(base, moved, amount):
        return base[amount * FINE :] + moved[: base.shape[0] - amount * FINE]

    tiles = [tall[:, i * LANES : (i + 1) * LANES] for i in range(3)]
    add_group(total, fold_lanes(tiles, shift), group, 48)


def fused_backward_kernel(
    dims,
    weight, wide, down, patches, probs, grad_final,
    gains, front_slope, unit_front, inverse_front, projected, attended, unit_middle, inverse_middle,
    middle_low, slope, activated, last_gain_grad,
    conv_out, qkv_out, out_out, up_out, down_out, gain_out, both_grads, *scratch,
):
    arrays = CONV + 1
    n = CONV + CONV_PARTS
    stages, pairs = scratch[:arrays], scratch[arrays : 2 * arrays]
    hops = [scratch[2 * arrays + level * n : 2 * arrays + (level + 1) * n] for level in range(3)]
    conv_rows = [pl.ds(i * (384 // CONV_PARTS), 384 // CONV_PARTS) for i in range(CONV_PARTS)]

    def in_parts(refs):
        return list(refs[:CONV]) + [refs[CONV].at[:, rows] for rows in conv_rows]

    outs = [down_out, up_out, out_out, qkv_out, gain_out] + [conv_out.at[rows] for rows in conv_rows]
    (
        grad, turned, grad_attended, grad_projected, padded, spread, tall, total, gain_grads, gain_wide,
        gain_box, tall_box, wide_box, tall_tiles, wide_tiles, prob_tiles, patch_tiles,
        pair_recv, hop_send, hop_recv, last_send, last_recv, box_sems, tile_sems, load_sems,
    ) = scratch[2 * arrays + 3 * n :]
    core_index = lax.axis_index("seq")
    other = 1 - core_index
    pack, width = grad.shape
    inner = activated.shape[1]
    low = jnp.bfloat16
    heights = [out.shape[0] for out in outs]
    scatter = Scatter(
        dims, heights, in_parts(stages), in_parts(pairs), hops, outs, pairs[CONV],
        (pair_recv, hop_send, hop_recv, last_send, last_recv),
    )
    tall_stream, wide_stream = Stream(tall_tiles, tile_sems.at[0]), Stream(wide_tiles, tile_sems.at[1])
    prob_stream, patch_stream = Stream(prob_tiles, tile_sems.at[2]), Stream(patch_tiles, tile_sems.at[3])
    tall_out, wide_out_box = Outbox(tall_box, box_sems.at[0]), Outbox(wide_box, box_sems.at[1])

    def strip(index, base=0):
        return pl.ds(pl.multiple_of(base + index * STRIP, LANES), STRIP)

    up_base, out_base = 4 * width, 3 * width
    load = pltpu.make_async_copy(grad_final, grad, load_sems.at[0])
    load.start()
    up_half, qkv_half, out_half = inner // 2, 3 * width // 2, width // 2
    up_strips, qkv_strips = up_half // STRIP, qkv_half // STRIP
    down_strips = inner // STRIP

    def ordered(index, strips):
        return jnp.where(index < strips, other * strips + index, core_index * strips + index - strips)

    def up_start(index):
        which = ordered(index, up_strips)
        wide_stream.start(wide.at[:, strip(which, up_base)], index)
        tall_stream.start(down.at[strip(which)], index)

    up_start(0)
    greet(dims, scatter.position, core_index)
    load.wait()

    def all_tasks(*wanted):
        return [[task for chunk, stage in wanted for task in scatter.tasks(core, chunk, stage)] for core in range(2)]

    def step(number):
        wanted = [(number - stage, stage) for stage in range(4) if 0 <= number - stage < n]
        return all_tasks(*wanted)

    def gate(chunk, count, height, lanes):
        for index in range(count):
            ref = pairs[chunk].at[pl.ds(0, height), pl.ds(0, lanes)]
            pltpu.make_async_copy(ref, ref, pair_recv.at[chunk, index]).wait()

    own_lanes = pl.ds(pl.multiple_of(core_index * out_half, LANES), out_half)
    other_lanes = pl.ds(pl.multiple_of(other * out_half, LANES), out_half)
    grad_feed = grad[...].astype(low)
    for index in range(down_strips):
        slot, box = tall_out.free()
        box[...] = dot(activated[:, index * STRIP : (index + 1) * STRIP], grad_feed, (0, 0)).astype(low)
        rows = pl.ds(index * STRIP, STRIP)
        tall_out.send(slot, box.at[:, other_lanes], pairs[DOWN].at[rows], pair_recv.at[DOWN, index])
        stages[DOWN][rows, :] = box[:, own_lanes]
    turned[...] = jnp.transpose(middle_low[...].astype(jnp.float32)).astype(low)
    gate(DOWN, down_strips, STRIP, out_half)
    spread[0:pack, :] = grad_feed

    def give(chunk, index, strips, values):
        if index < strips:
            slot, box = wide_out_box.free()
            box[...] = values
            lanes = pl.ds(index * STRIP, STRIP)
            wide_out_box.send(slot, box, pairs[chunk].at[:, lanes], pair_recv.at[chunk, index])
        else:
            stages[chunk][:, (index - strips) * STRIP : (index - strips + 1) * STRIP] = values

    def up_piece(index):
        def piece():
            if index + 1 < 2 * up_strips:
                up_start(index + 1)
            up_tile, down_tile = wide_stream.take(index), tall_stream.take(index)
            lanes = strip(ordered(index, up_strips))
            slopes = slope[:, lanes].astype(jnp.float32)
            grad_hidden = (dot(spread[0:pack, :], down_tile[...], (1, 1)) * slopes).astype(low)
            give(UP, index, up_strips, dot(turned[...], grad_hidden).astype(low))
            grad[...] += dot(grad_hidden, up_tile[...], (1, 1))

        return piece

    weave(step(0), [up_piece(i) for i in range(2 * up_strips)])

    def prob_start(pair):
        prob_stream.start(probs.at[pl.ds(2 * pair, 2)], pair)

    for index in range(2):
        tall_stream.start(wide.at[strip(index), out_base : out_base + width], index)
    prob_start(0)
    gain_grads[...] = last_gain_grad[...]

    def middle_piece():
        gate(UP, up_strips, width, STRIP)
        norm_back_rows(grad, unit_middle, inverse_middle, gains, 1, gain_grads)

    def out_piece():
        grad_branch = grad[...].astype(low)
        spread[0:pack, :] = grad_branch
        turned[...] = jnp.transpose(attended[...].astype(jnp.float32)).astype(low)
        for index, half in enumerate((other, core_index)):
            give(OUT, index, 1, dot(turned[...], spread[0:pack, strip(half)]).astype(low))
            tile = tall_stream.take(index)
            lanes = slice(index * STRIP, (index + 1) * STRIP)
            grad_attended[:, lanes] = dot(grad_branch, tile[...], (1, 1)).astype(low)

    pairs_of_heads = width // LANES

    def attend_piece(pair):
        def piece():
            if pair + 1 < pairs_of_heads:
                prob_start(pair + 1)
            attend_back_pair(projected, grad_attended, prob_stream.take(pair), grad_projected, pair)

        return piece

    def qkv_start(index):
        wide_stream.start(wide.at[:, strip(ordered(index, qkv_strips))], index)

    def qkv_piece(index):
        def piece():
            if index == 0:
                qkv_start(0)
                turned[...] = jnp.transpose(unit_front[...] * gains[0:1, :]).astype(low)
            if index + 1 < 2 * qkv_strips:
                qkv_start(index + 1)
            tile = wide_stream.take(index)
            values = grad_projected[:, strip(ordered(index, qkv_strips))]
            give(QKV, index, qkv_strips, dot(turned[...], values).astype(low))
            grad[...] += dot(values, tile[...], (1, 1))

        return piece

    places = sorted(offsets_of(dims), key=lambda o: (o[1] == 0) + (o[2] == 0))
    groups = [place(dims, (0, 1, 2), scatter.position, offsets) for offsets in places]

    def conv_start(number):
        tall_stream.start(weight.at[groups[number]], number)
        patch_stream.start(patches.at[groups[number]], number)

    def front_piece():
        conv_start(0)
        norm_back_rows(grad, unit_front, inverse_front, gains, 0, gain_grads)
        padded[...] = jnp.zeros_like(padded)
        tall[...] = jnp.zeros_like(tall)
        total[...] = jnp.zeros_like(total)
        total[:, :width] = grad[...]

        def body(rows):
            padded[rows, 0:width] = (grad[rows, :] * front_slope[rows, :]).astype(low).astype(jnp.float32)

        row_tiles(pack, body)
        gain_wide[...] = jnp.zeros_like(gain_wide)
        gain_wide[0:8, 0:width] = gain_grads[...]

        @pl.loop(0, scatter.count)
        def _(shard):
            one = take_group(gain_wide, slice(0, 16), shard, width // scatter.count)
            gain_box[shard] = one.astype(low)
            stages[GAIN][shard] = one.astype(low)

        gain_copy.start()

    gain_copy = pltpu.make_async_remote_copy(
        src_ref=gain_box,
        dst_ref=pairs[GAIN],
        send_sem=load_sems.at[1],
        recv_sem=load_sems.at[2],
        device_id={"seq": other},
        device_id_type=MESH,
    )

    def conv_piece(number):
        def piece():
            if number + 1 < len(groups):
                conv_start(number + 1)
            group = groups[number]
            tile, patch = tall_stream.take(number), patch_stream.take(number)
            spread[...] = spread_grads(padded, group, pack)
            slot, box = tall_out.free()
            box[...] = dot(patch[...], spread[...], (0, 0)).astype(low)
            tall_out.send(slot, box.at[:, other_lanes], pairs[CONV].at[group], pair_recv.at[CONV, group])
            stages[CONV][group] = box[:, own_lanes]
            add_backward(total, tall, spread[...], tile[...], group, pack)

        return piece

    middle_piece()
    weave(
        step(1),
        [out_piece]
        + [attend_piece(i) for i in range(pairs_of_heads)]
        + [qkv_piece(i) for i in range(2 * qkv_strips)]
        + [front_piece],
    )
    pieces = [conv_piece(i) for i in range(len(groups))]
    gate(OUT, 1, width, STRIP)
    weave(step(2), pieces[:7])
    gate(QKV, qkv_strips, width, STRIP)
    weave(step(3), pieces[7:14])
    gain_copy.wait()
    weave(step(4), pieces[14:])
    half = pack // 2
    here = pl.ds(pl.multiple_of(core_index * half, half), half)
    there = pl.ds(pl.multiple_of(other * half, half), half)
    frames_copy = pltpu.make_async_remote_copy(
        src_ref=total.at[there, pl.ds(0, width)],
        dst_ref=both_grads.at[core_index],
        send_sem=load_sems.at[3],
        recv_sem=load_sems.at[4],
        device_id={"seq": other},
        device_id_type=MESH,
    )
    frames_copy.start()
    both_grads[core_index] = total[here, 0:width]
    for number in range(5, n + 3):
        weave(step(number), [])
    by_core(core_index, scatter.finish)
    tall_out.drain()
    wide_out_box.drain()
    frames_copy.wait()


def fused_backward(weight, wide, down, patches, gains, kept, dp):
    dims = dp_factors(dp)
    (front_slope, grad_final, unit_front, inverse_front, projected, probs, attended, unit_middle,
     inverse_middle, middle_low, slope, activated, gain_grads) = kept
    pack, width = front_slope.shape
    inner = activated.shape[1]
    low, full = jnp.bfloat16, jnp.float32
    shape = jax.ShapeDtypeStruct
    vmem = pl.BlockSpec(memory_space=pltpu.VMEM)
    any_ = pl.BlockSpec(memory_space=pl.ANY)
    rows = width // dp
    flat = [(inner, width // 2), (width, inner // 2), (width, width // 2), (width, 3 * width // 2)]
    wholes = flat + [(dp, 16, LANES), (dp, 384, 384)]
    blocks = [(s[0] // dp, s[1]) for s in flat] + [(16, LANES)] + [(384 // CONV_PARTS, 384)] * CONV_PARTS
    n = len(blocks)
    scratch = [pltpu.VMEM(s, low) for s in wholes] * 2
    for level in range(3):
        for block, orders in zip(blocks, SCATTER_ORDERS):
            slots = max(hop_slots(dims, order)[level] for order in orders)
            scratch.append(pltpu.VMEM((slots,) + block, low))
    tall_rows = pack + FINE
    scratch += [
        pltpu.VMEM((pack, width), full),
        pltpu.VMEM((width, pack), low),
        pltpu.VMEM((pack, width), low),
        pltpu.VMEM((pack, 3 * width), low),
        pltpu.VMEM((tall_rows, width + LANES), full),
        pltpu.VMEM((tall_rows, width), low),
        pltpu.VMEM((pack + KERNEL - FINE, 384), full),
        pltpu.VMEM((pack, width + LANES), full),
        pltpu.VMEM((8, width), full),
        pltpu.VMEM((16, width + LANES), full),
        pltpu.VMEM((dp, 16, LANES), low),
        pltpu.VMEM((2, STRIP, width), low),
        pltpu.VMEM((2, width, STRIP), low),
        pltpu.VMEM((2, STRIP, width), low),
        pltpu.VMEM((2, width, STRIP), low),
        pltpu.VMEM((2, 2, pack, pack), full),
        pltpu.VMEM((2, tall_rows, 384), low),
        pltpu.SemaphoreType.DMA((n, dp)),
        pltpu.SemaphoreType.DMA((n, dp)),
        pltpu.SemaphoreType.DMA((n, dp)),
        pltpu.SemaphoreType.DMA((n,)),
        pltpu.SemaphoreType.DMA((n,)),
        pltpu.SemaphoreType.DMA((2, 2)),
        pltpu.SemaphoreType.DMA((4, 2)),
        pltpu.SemaphoreType.DMA((5,)),
    ]
    return pl.pallas_call(
        functools.partial(fused_backward_kernel, dims),
        out_shape=[
            shape((384, width), full),
            shape((rows, 3 * width), full),
            shape((rows, width), full),
            shape((rows, inner), full),
            shape((inner // dp, width), full),
            shape((16, 2 * LANES), full),
            shape((2, pack // 2, width), full),
        ],
        in_specs=[any_] * 6 + [vmem] * 12,
        out_specs=[vmem] * 7,
        scratch_shapes=scratch,
        compiler_params=pltpu.CompilerParams(
            collective_id=3, has_side_effects=True, vmem_limit_bytes=63 << 20
        ),
    )(weight, wide, down, patches, probs, grad_final, gains, front_slope, unit_front, inverse_front,
      projected, attended, unit_middle, inverse_middle, middle_low, slope, activated, gain_grads)


GAIN_ROWS = 16


def chunks_of(conv_rows, conv_lanes, wide_rows, width, down_rows):
    both = range(2)
    quarter, half = conv_rows // 4, width // 2
    conv = [
        [(0, ((2 * part + core) * quarter, quarter), (0, conv_lanes)) for core in both] for part in both
    ]
    wide = [
        [(1, (0, wide_rows), ((2 * part + core) * 2 * width, 2 * width)) for core in both] for part in both
    ]
    down = [[(2, (0, down_rows), (core * half, half)) for core in both]]
    gain = [[(3, (core * GAIN_ROWS, GAIN_ROWS), (0, LANES)) for core in both]]
    return gain, conv, wide, down


def gather_chunks(chunks):
    return [
        (FIRST,) + tuple((array, array, rows, lanes[0], lanes[0], lanes[1]) for array, rows, lanes in chunk)
        for chunk in chunks
    ]


def fused_chunks(conv_rows, width, wide_rows, inner, down_rows):
    quarter = conv_rows // 4
    chunks = [(FIRST,) + tuple((5, 3, (core * GAIN_ROWS, GAIN_ROWS), 0, 0, LANES) for core in range(2))]
    for part, orders in enumerate((FIRST, FIRST)):
        chunks.append(
            (orders,) + tuple((0, 0, ((2 * part + core) * quarter, quarter), 0, 0, width) for core in range(2))
        )
    begin = 0
    for source, lanes, orders in ((1, 3 * width, FIRST), (2, width, FIRST), (3, inner, SECOND)):
        half = lanes // 2
        chunks.append(
            (orders,)
            + tuple((source, 1, (0, wide_rows), core * half, begin + core * half, half) for core in range(2))
        )
        begin += lanes
    half = width // 2
    chunks.append(
        (FIRST,) + tuple((4, 2, (0, down_rows), core * half, core * half, half) for core in range(2))
    )
    return chunks


def shards(
    frames,
    clip_lengths,
    conv_weight,
    front_gain,
    qkv_weight,
    out_weight,
    middle_gain,
    up_weight,
    down_weight,
    final_gain,
    cotangent,
):
    dp = lax.axis_size("dp")
    low = jnp.bfloat16
    width = frames.shape[2]
    columns = conv_weight.shape[2]
    group_width = conv_weight.shape[1]
    gain_width = front_gain.shape[0]
    conv_shard = (
        conv_weight.reshape(COARSE, FINE, group_width, columns)
        .transpose(0, 2, 1, 3)
        .reshape(COARSE * group_width, FINE * columns)
    )
    split = group_width // columns
    if split == 1:
        shards_in = (conv_shard, qkv_weight, out_weight, up_weight, down_weight) + tuple(
            gain[None] for gain in (front_gain, middle_gain, final_gain)
        )
        chunks = fused_chunks(conv_shard.shape[0], width, qkv_weight.shape[0], up_weight.shape[1], down_weight.shape[0])
        (weight, wide, down, patches, front_slope, unit_front, projected, probs, attended, unit_middle, middle_low,
         outputs, gains, grad_final, inverse_front, inverse_middle, slope, activated, last_gain_grad) = fused_forward(
            frames, cotangent, clip_lengths[:, 0], shards_in, chunks, dp
        )
        kept = (front_slope, grad_final, unit_front, inverse_front, projected, probs, attended, unit_middle,
                inverse_middle, middle_low, slope, activated, last_gain_grad)
    else:
        wide_shard = jnp.concatenate([qkv_weight, out_weight, up_weight], axis=1)
        gain_shard = jnp.pad(
            jnp.stack([front_gain, middle_gain, final_gain]),
            ((0, 2 * GAIN_ROWS - 3), (0, LANES - gain_width)),
        )
        parts = (conv_shard, wide_shard, down_weight, gain_shard)
        gain_chunk, conv_chunks, wide_chunks, down_chunk = chunks_of(
            *conv_shard.shape, wide_shard.shape[0], width, down_weight.shape[0]
        )
        chunks = gather_chunks(gain_chunk + conv_chunks + wide_chunks + down_chunk)
        conv_all, wide_all, down_all, gain_all = all_gather(parts, chunks, dp)
        weight = (
            conv_all.reshape(GROUPS, split, COARSE * group_width, FINE, columns)
            .transpose(0, 2, 3, 1, 4)
            .reshape(GROUPS, COARSE * group_width, FINE * group_width)
        )
        wide = wide_all.reshape(width, wide_shard.shape[1])
        down = down_all.reshape(-1, width)
        gains = gain_all[:, :3, :gain_width].transpose(1, 0, 2).reshape(3, width).astype(jnp.float32)
        gains = jnp.pad(gains, ((0, 5), (0, 0)))
        both = lax.all_to_all(
            jnp.stack([frames, cotangent], axis=1), "seq", split_axis=0, concat_axis=2, tiled=True
        )
        pack_frames, pack_cotangent = both[0, 0], both[0, 1]
        lengths = lax.dynamic_index_in_dim(clip_lengths[:, 0], lax.axis_index("seq"), 0)
        convolved, patches = conv_forward(pack_frames, weight)
        output, *kept = middle_forward(
            pack_frames, convolved, lengths, gains, wide, down, pack_cotangent
        )
        outputs = lax.all_to_all(output[None], "seq", split_axis=1, concat_axis=0, tiled=True)

    if split == 1:
        conv_sum, qkv_sum, out_sum, up_sum, down_sum, gain_sum, frame_grads = fused_backward(
            weight, wide, down, patches, gains, kept, dp
        )
    else:
        grad_mixed, grad_convolved, wide_grad, down_grad, gain_grads = middle_backward(
            gains, wide, down, kept
        )
        frame_grad, conv_grad = conv_backward(grad_convolved, grad_mixed, weight, patches)

        conv_blocks = (
            conv_grad.reshape(GROUPS, COARSE * group_width, FINE, split, columns)
            .transpose(0, 3, 1, 2, 4)
            .reshape((dp,) + conv_shard.shape)
        )
        gain_blocks = jnp.pad(
            gain_grads[:3].astype(low).reshape(3, dp, gain_width).transpose(1, 0, 2),
            ((0, 0), (0, 2 * GAIN_ROWS - 3), (0, LANES - gain_width)),
        )
        conv_sum, wide_sum, down_sum, gain_sum = reduce_scatter(
            (
                conv_blocks,
                wide_grad.reshape((dp,) + wide_shard.shape),
                down_grad.reshape((dp,) + down_weight.shape),
                gain_blocks,
            ),
            gain_chunk + down_chunk + wide_chunks[::-1] + conv_chunks,
            dp,
        )
        qkv_sum, out_sum, up_sum = (
            wide_sum[:, : 3 * width],
            wide_sum[:, 3 * width : 4 * width],
            wide_sum[:, 4 * width :],
        )
        frame_grads = lax.all_to_all(frame_grad[None], "seq", split_axis=1, concat_axis=0, tiled=True)

    conv_sum = (
        conv_sum.reshape(COARSE, group_width, FINE, columns)
        .transpose(0, 2, 1, 3)
        .reshape(conv_weight.shape)
    )
    return (
        outputs,
        frame_grads,
        conv_sum,
        gain_sum[0, :gain_width],
        qkv_sum,
        out_sum,
        gain_sum[1, :gain_width],
        up_sum,
        down_sum,
        gain_sum[2, :gain_width],
    )


def solution(mesh):
    frames_spec = P(None, ("dp", "seq"), None)
    row, matrix, columns = P("dp"), P("dp", None), P(None, None, "dp")
    return jax.shard_map(
        shards,
        mesh=mesh,
        in_specs=(
            frames_spec,
            P(None, "dp", None),
            columns,
            row,
            matrix,
            matrix,
            row,
            matrix,
            matrix,
            row,
            frames_spec,
        ),
        out_specs=(
            frames_spec,
            frames_spec,
            columns,
            row,
            matrix,
            matrix,
            row,
            matrix,
            matrix,
            row,
        ),
        check_vma=False,
    )
```

profile of v0, /device:TPU:0, one launch (start us, length us, event | category | flops | bytes accessed | tf_op | source)
XLA Modules:
  0.0 283.5 jit_solution(17355951803356258265)
XLA Ops:
  0.6 1.8 copy.23
  2.5 0.4 copy.24
  2.9 2.3 reshape.33.conv_shard
  5.2 127.2 %shard_map.186 = (bf16[16,384,768]{2,1,0:T(8,128)(2,1)}, bf16[768,6144]{1,0:T(8,128)(2,1)}, bf16[3072,768]{1,0:T(8,128)(2,1)}, bf16[16,272,384]{2,1,0:T(8,128)(2...) custom-call(s32[2,3]{1,0:T(2,128)} %bitcast.20, ...), custom_call_target="tpu_custom_call" | custom-call | tf_op jit(solution)/shard_map/pallas_call | solution.py:1201
  132.4 136.0 %shard_map.187 = (f32[384,768]{1,0:T(8,128)}, f32[48,2304]{1,0:T(8,128)}, f32[48,768]{1,0:T(8,128)}, f32[48,3072]{1,0:T(8,128)}, f32[192,768]{1,0:T(8,128)}, /*index=5*/f32[16,256]{1,0:T(8,128)}, f32[2,128,768]{2,1,0:T(8,128)}) custom-call(bf16[16,384,768]{2,1,0:T(8,128)(2,1)} %get-tuple-element.37.weight, bf16[768,6144]{1,0:T(8,128)(2,1)} %get-tuple-element.38.wide, ...), custom_call_target="tpu_custom_call" | custom-call | tf_op jit(solution)/shard_map/pallas_call | solution.py:1729
  268.4 1.3 slice_bitcast_fusion
  269.7 2.6 reshape.34
  272.4 2.6 copy.25
  275.0 0.0 copy-start.4
  275.0 0.0 copy-start
  275.0 0.0 copy-start.2
  275.0 3.3 %copy.26 = f32[128,48,48]{0,2,1:T(8,128)} copy(f32[128,48,48]{2,1,0:T(8,128)} %bitcast.18) | data formatting | bytes 2359296
  278.3 0.0 copy-done.4
  278.3 0.7 copy.33
  279.1 0.0 copy-done
  279.1 0.9 copy.34
  279.9 0.0 copy-done.3
  279.9 0.8 copy.35
  280.7 0.0 copy-done.5
  280.7 0.7 copy.36
  281.4 0.0 copy-done.2
  281.4 0.8 copy.37
  282.2 0.0 copy-done.1
  282.2 0.8 copy.38
  (3 shorter events, 0.0 us)
Async XLA Ops:
  275.0 3.4 %copy-start.4 = (bf16[2,128,768]{2,1,0:T(8,128)(2,1)S(1)}, bf16[2,128,768]{2,1,0:T(8,128)(2,1)}, u32[]{:S(2)}) copy-start(bf16[2,128,768]{2,1,0:T(8,128)(2,1)} %get-tuple-element.85) | copy-start | bytes 1179652
  275.0 4.1 %copy-start = (f32[2,128,768]{2,1,0:T(8,128)S(1)}, f32[2,128,768]{2,1,0:T(8,128)}, u32[]{:S(2)}) copy-start(f32[2,128,768]{2,1,0:T(8,128)} %get-tuple-element.86) | copy-start | bytes 2359300
  275.0 5.0 %copy-start.3 = (f32[48,2304]{1,0:T(8,128)S(1)}, f32[48,2304]{1,0:T(8,128)}, u32[]{:S(2)}) copy-start(f32[48,2304]{1,0:T(8,128)} %get-tuple-element.89) | copy-start | bytes 1327108
  275.0 5.7 %copy-start.5 = (f32[48,768]{1,0:T(8,128)S(1)}, f32[48,768]{1,0:T(8,128)}, u32[]{:S(2)}) copy-start(f32[48,768]{1,0:T(8,128)} %get-tuple-element.90) | copy-start | bytes 442372
  275.0 6.4 %copy-start.2 = (f32[48,3072]{1,0:T(8,128)S(1)}, f32[48,3072]{1,0:T(8,128)}, u32[]{:S(2)}) copy-start(f32[48,3072]{1,0:T(8,128)} %get-tuple-element.92) | copy-start | bytes 1769476
  278.3 3.9 %copy-start.1 = (f32[192,768]{1,0:T(8,128)S(1)}, f32[192,768]{1,0:T(8,128)}, u32[]{:S(2)}) copy-start(f32[192,768]{1,0:T(8,128)} %get-tuple-element.93) | copy-start | bytes 1769476
where the time goes:
time: 289 us; the launch traced here: 283 us
  Pallas kernels  263 us (91%)
  local copies, waits for them, and re-layouts  19.1 us (7%)
    pallas_call x1, Pallas kernels, fused_backward(): pl.pallas_call(functools.partial(fused_backward_kernel, dims), out_shape=...  136 us
    pallas_call x1, Pallas kernels, fused_forward(): pl.pallas_call(functools.partial(fused_forward_kernel, dims, chunks), out...  127 us
    unnamed x20, local copies, waits for them, and re-layouts  9.88 us

commit v1 on v0

--- a/solution.py
+++ b/solution.py
@@ -743,6 +743,10 @@
         middle[...] += dot(activated[:, lanes], weight[lanes, :])
 
     lane_tiles(activated.shape[1] // TILE, body)
+    last_norm(middle, gains, cotangent, output, grad_final, gain_grads)
+
+
+def last_norm(middle, gains, cotangent, output, grad_final, gain_grads):
     gain_grads[2:3, :] = jnp.zeros((1, middle.shape[1]), jnp.float32)
 
     def finish(rows):
@@ -969,9 +973,10 @@
     lengths, frames, cotangent, conv_shard, qkv_shard, out_shard, up_shard, down_shard, front_gain, middle_gain,
     final_gain,
     conv_out, wide_out, down_out, patches_out, front_slope_out, unit_front_out, projected_out, probs_out,
-    attended_out, unit_middle_out, middle_low_out, both_output, gains, grad_final, inverse_front, inverse_middle,
-    slope, activated, gain_grads,
-    patches, front_slope, unit_front, projected, probs, attended, unit_middle, middle_low, gain_shard,
+    attended_out, unit_middle_out, middle_low_out, slope_out, activated_out, both_output, gains, grad_final,
+    inverse_front, inverse_middle, gain_grads,
+    patches, front_slope, unit_front, projected, probs, attended, unit_middle, middle_low, slope, activated,
+    gain_shard,
     conv_all, wide_all, down_all, gain_all, pack_frames, pack_cotangent, output, padded, total,
     gains_wide, normed, normed_low, middle,
     send_sems, recv_sems, push_send, push_recv, own_sems, local_sems, save_sems, pair_sems,
@@ -1025,11 +1030,11 @@
         both = []
         for core in range(2):
             tasks = []
+            for stage in (3, 2, 1):
+                if 0 <= step - stage < len(chunks):
+                    tasks += gather.tasks(core, step - stage, stage)
             if 3 <= step + 2 < len(chunks):
                 tasks += gather.tasks(core, step + 2, 0)
-            for stage in (1, 2, 3):
-                if 0 <= step - stage < len(chunks):
-                    tasks += gather.tasks(core, step - stage, stage)
             both.append(tasks)
         steps.append(both)
 
@@ -1079,17 +1084,8 @@
         copy.wait()
     conv_pieces = [conv_piece(offsets) for offsets in places]
     alone = sum(1 for offsets in places if not (offsets[1] or offsets[2]))
-    pairs = sum(1 for offsets in places if offsets[1] and offsets[2])
-    weave(steps[3], conv_pieces[:alone])
-    last = len(gather.tasks(0, 2, 3))
-    weave([tasks[:-last] for tasks in steps[4]], [])
-    taken = alone
-    for number in range(last):
-        many = 1 if number >= last - pairs else (len(places) - alone - pairs) // (last - pairs)
-        weave([tasks[number - last :][:1] for tasks in steps[4]], [])
-        for piece in conv_pieces[taken : taken + many]:
-            piece()
-        taken += many
+    weave(steps[3], [])
+    weave(steps[4], conv_pieces[:alone])
     gate(0)
     saves = []
 
@@ -1099,7 +1095,6 @@
         saves.append(copy)
 
     save(patches, patches_out)
-    save(conv_all, conv_out)
     gains_wide[...] = jnp.zeros_like(gains_wide)
 
     @pl.loop(0, gather.count)
@@ -1108,6 +1103,7 @@
 
     gains[...] = gains_wide[0:8, 0:width]
     def front_piece():
+        save(conv_all, conv_out)
         front_norm(pack_frames, total, gains, normed, normed_low, unit_front, inverse_front, front_slope)
         save(front_slope, front_slope_out)
         save(unit_front, unit_front_out)
@@ -1132,8 +1128,13 @@
         save(middle_low, middle_low_out)
 
     head_pairs = width // LANES
-    weave(steps[5], [front_piece])
-    weave(steps[6], [project_piece] + [attend_piece(i, i + 2) for i in range(0, head_pairs, 2)])
+    weave(steps[5], conv_pieces[alone : 3 * alone])
+    weave(
+        steps[6],
+        conv_pieces[3 * alone :]
+        + [front_piece, project_piece]
+        + [attend_piece(i, i + 2) for i in range(0, head_pairs, 2)],
+    )
     weave(steps[7], [middle_piece])
     up = wide_all.at[:, 4 * width :]
     count = slope.shape[1] // TILE
@@ -1148,13 +1149,34 @@
 
         return piece
 
-    weave(steps[8], [up_piece(i) for i in range(0, count, third)])
-    gate(6)
-    save(down_all, down_out)
+    arrivals = [(i, j) for j in [0] + near_first(dims[1]) for i in rank]
+    down_tasks = steps[8]
+    near = len(rank)
+
+    def strip_piece(offsets):
+        gids = [place(dims, (0, 1, 2), gather.position, offsets + (k,)) for k in range(2)]
+
+        def wait(core):
+            for k, gid in enumerate(gids):
+                if offsets + (k,) != (0, 0, 0):
+                    gather.arrived_block(core, 6, gid)
+
+        by_core(core_index, wait)
+        rows = pl.ds(pl.multiple_of(gids[0] // 2 * STRIP, STRIP), STRIP)
+        save(down_all.at[rows], down_out.at[rows])
+        middle[...] += dot(activated[:, rows], down_all[rows, :])
+
+    weave([tasks[:near] for tasks in down_tasks], [up_piece(i) for i in range(0, count, third)])
+    save(slope, slope_out)
+    save(activated, activated_out)
     for copy in moves[2:]:
         copy.wait()
     gain_grads[...] = jnp.zeros_like(gain_grads)
-    feed_down(activated, down_all, middle, gains, pack_cotangent, output, grad_final, gain_grads)
+    for number, offsets in enumerate(arrivals):
+        if number >= near:
+            weave([tasks[number : number + 1] for tasks in down_tasks], [])
+        strip_piece(offsets)
+    last_norm(middle, gains, pack_cotangent, output, grad_final, gain_grads)
     last = to_partner(output.at[there], both_output.at[core_index], 2)
     last.start()
     stay = pltpu.make_async_copy(output.at[here], both_output.at[core_index], local_sems.at[2])
@@ -1187,6 +1209,8 @@
         shape((pack, width), low),
         shape((pack, width), full),
         shape((pack, width), low),
+        shape((pack, inner), low),
+        shape((pack, inner), low),
     ]
     saved = [
         shape(frames.shape, low),
@@ -1194,15 +1218,13 @@
         shape((pack, width), full),
         shape((pack, LANES), full),
         shape((pack, LANES), full),
-        shape((pack, inner), low),
-        shape((pack, inner), low),
         shape((8, width), full),
     ]
     return pl.pallas_call(
         functools.partial(fused_forward_kernel, dims, chunks),
         out_shape=[shape(conv_shape, low), shape(wide_shape, low), shape(down_shape, low)] + kept + saved,
         in_specs=[pl.BlockSpec(memory_space=pltpu.SMEM)] + [any_] * 7 + [vmem] * 3,
-        out_specs=[any_] * 11 + [vmem] * len(saved),
+        out_specs=[any_] * 13 + [vmem] * len(saved),
         scratch_shapes=[pltpu.VMEM(one.shape, one.dtype) for one in kept]
         + [
             pltpu.VMEM((2 * GAIN_ROWS, LANES), low),
@@ -1225,7 +1247,7 @@
             pltpu.SemaphoreType.DMA((n, dp)),
             pltpu.SemaphoreType.DMA((n, 2)),
             pltpu.SemaphoreType.DMA((3,)),
-            pltpu.SemaphoreType.DMA((11,)),
+            pltpu.SemaphoreType.DMA((20,)),
             pltpu.SemaphoreType.DMA((2, 3)),
         ],
         compiler_params=pltpu.CompilerParams(
@@ -1434,9 +1456,9 @@
 
 def fused_backward_kernel(
     dims,
-    weight, wide, down, patches, probs, grad_final,
-    gains, front_slope, unit_front, inverse_front, projected, attended, unit_middle, inverse_middle,
-    middle_low, slope, activated, last_gain_grad,
+    weight, wide, down, patches, probs, grad_in, activated_in, middle_low_in, slope_in, unit_middle_in, attended_in,
+    projected_in, unit_front_in, front_slope_in,
+    gains, inverse_front, inverse_middle, last_gain_grad,
     conv_out, qkv_out, out_out, up_out, down_out, gain_out, both_grads, *scratch,
 ):
     arrays = CONV + 1
@@ -1450,9 +1472,10 @@
 
     outs = [down_out, up_out, out_out, qkv_out, gain_out] + [conv_out.at[rows] for rows in conv_rows]
     (
-        grad, turned, grad_attended, grad_projected, padded, spread, tall, total, gain_grads, gain_wide,
+        grad, activated, middle_low, slope, unit_middle, attended, projected, unit_front, front_slope,
+        turned, grad_attended, grad_projected, padded, spread, tall, total, gain_grads, gain_wide,
         gain_box, tall_box, wide_box, tall_tiles, wide_tiles, prob_tiles, patch_tiles,
-        pair_recv, hop_send, hop_recv, last_send, last_recv, box_sems, tile_sems, load_sems,
+        pair_recv, hop_send, hop_recv, last_send, last_recv, box_sems, tile_sems, load_sems, input_sems,
     ) = scratch[2 * arrays + 3 * n :]
     core_index = lax.axis_index("seq")
     other = 1 - core_index
@@ -1472,14 +1495,21 @@
         return pl.ds(pl.multiple_of(base + index * STRIP, LANES), STRIP)
 
     up_base, out_base = 4 * width, 3 * width
-    load = pltpu.make_async_copy(grad_final, grad, load_sems.at[0])
-    load.start()
+    sources = (grad_in, activated_in, middle_low_in, slope_in, unit_middle_in, attended_in, projected_in,
+               unit_front_in, front_slope_in)
+    targets = (grad, activated, middle_low, slope, unit_middle, attended, projected, unit_front, front_slope)
+    loads = [
+        pltpu.make_async_copy(source, target, input_sems.at[i])
+        for i, (source, target) in enumerate(zip(sources, targets))
+    ]
+    for load in loads:
+        load.start()
     up_half, qkv_half, out_half = inner // 2, 3 * width // 2, width // 2
     up_strips, qkv_strips = up_half // STRIP, qkv_half // STRIP
     down_strips = inner // STRIP
 
     def ordered(index, strips):
-        return jnp.where(index < strips, other * strips + index, core_index * strips + index - strips)
+        return (core_index if index % 2 else other) * strips + index // 2
 
     def up_start(index):
         which = ordered(index, up_strips)
@@ -1488,13 +1518,14 @@
 
     up_start(0)
     greet(dims, scatter.position, core_index)
-    load.wait()
 
     def all_tasks(*wanted):
         return [[task for chunk, stage in wanted for task in scatter.tasks(core, chunk, stage)] for core in range(2)]
 
     def step(number):
-        wanted = [(number - stage, stage) for stage in range(4) if 0 <= number - stage < n]
+        wanted = [(number - stage, stage) for stage in (3, 2, 1, 0) if 0 < number - stage < n]
+        if number < 3:
+            wanted.insert(0, (DOWN, number + 1))
         return all_tasks(*wanted)
 
     def gate(chunk, count, height, lanes):
@@ -1504,25 +1535,45 @@
 
     own_lanes = pl.ds(pl.multiple_of(core_index * out_half, LANES), out_half)
     other_lanes = pl.ds(pl.multiple_of(other * out_half, LANES), out_half)
+    loads[0].wait()
+    loads[1].wait()
     grad_feed = grad[...].astype(low)
-    for index in range(down_strips):
-        slot, box = tall_out.free()
-        box[...] = dot(activated[:, index * STRIP : (index + 1) * STRIP], grad_feed, (0, 0)).astype(low)
-        rows = pl.ds(index * STRIP, STRIP)
-        tall_out.send(slot, box.at[:, other_lanes], pairs[DOWN].at[rows], pair_recv.at[DOWN, index])
-        stages[DOWN][rows, :] = box[:, own_lanes]
+    spread[0:pack, :] = grad_feed
+    first = [(i, j, 0) for j in near_first(dims[1]) + [0] for i in near_first(dims[0])[::-1] + [0]]
+    strips = [place(dims, (0, 1, 2), scatter.position, offsets) // 2 for offsets in first]
+    sends = [scatter.tasks(core, DOWN, 0) for core in range(2)]
+    ahead = len(strips) // 2
+    for index in range(down_strips + 1):
+        if index < down_strips:
+            slot, box = tall_out.free()
+            rows = strip(strips[index])
+            box[...] = dot(activated[:, rows], spread[0:pack, :], (0, 0)).astype(low)
+            tall_out.send(slot, box.at[:, other_lanes], pairs[DOWN].at[rows], pair_recv.at[DOWN, index])
+            stages[DOWN][rows, :] = box[:, own_lanes]
+        if index > 0:
+            came = pairs[DOWN].at[strip(strips[index - 1])]
+            pltpu.make_async_copy(came, came, pair_recv.at[DOWN, index - 1]).wait()
+
+            def early(core, index=index - 1):
+                if core == 0:
+                    sends[0][index]()
+                elif index < ahead:
+                    sends[1][index]()
+                    sends[1][index + ahead]()
+
+            by_core(core_index, early)
+    loads[2].wait()
+    loads[3].wait()
     turned[...] = jnp.transpose(middle_low[...].astype(jnp.float32)).astype(low)
-    gate(DOWN, down_strips, STRIP, out_half)
-    spread[0:pack, :] = grad_feed
-
-    def give(chunk, index, strips, values):
-        if index < strips:
+
+    def give(chunk, index, values):
+        lanes = pl.ds(index // 2 * STRIP, STRIP)
+        if index % 2 == 0:
             slot, box = wide_out_box.free()
             box[...] = values
-            lanes = pl.ds(index * STRIP, STRIP)
-            wide_out_box.send(slot, box, pairs[chunk].at[:, lanes], pair_recv.at[chunk, index])
+            wide_out_box.send(slot, box, pairs[chunk].at[:, lanes], pair_recv.at[chunk, index // 2])
         else:
-            stages[chunk][:, (index - strips) * STRIP : (index - strips + 1) * STRIP] = values
+            stages[chunk][:, lanes] = values
 
     def up_piece(index):
         def piece():
@@ -1532,7 +1583,7 @@
             lanes = strip(ordered(index, up_strips))
             slopes = slope[:, lanes].astype(jnp.float32)
             grad_hidden = (dot(spread[0:pack, :], down_tile[...], (1, 1)) * slopes).astype(low)
-            give(UP, index, up_strips, dot(turned[...], grad_hidden).astype(low))
+            give(UP, index, dot(turned[...], grad_hidden).astype(low))
             grad[...] += dot(grad_hidden, up_tile[...], (1, 1))
 
         return piece
@@ -1548,6 +1599,8 @@
     gain_grads[...] = last_gain_grad[...]
 
     def middle_piece():
+        for load in loads[4:]:
+            load.wait()
         gate(UP, up_strips, width, STRIP)
         norm_back_rows(grad, unit_middle, inverse_middle, gains, 1, gain_grads)
 
@@ -1556,7 +1609,7 @@
         spread[0:pack, :] = grad_branch
         turned[...] = jnp.transpose(attended[...].astype(jnp.float32)).astype(low)
         for index, half in enumerate((other, core_index)):
-            give(OUT, index, 1, dot(turned[...], spread[0:pack, strip(half)]).astype(low))
+            give(OUT, index, dot(turned[...], spread[0:pack, strip(half)]).astype(low))
             tile = tall_stream.take(index)
             lanes = slice(index * STRIP, (index + 1) * STRIP)
             grad_attended[:, lanes] = dot(grad_branch, tile[...], (1, 1)).astype(low)
@@ -1583,7 +1636,7 @@
                 qkv_start(index + 1)
             tile = wide_stream.take(index)
             values = grad_projected[:, strip(ordered(index, qkv_strips))]
-            give(QKV, index, qkv_strips, dot(turned[...], values).astype(low))
+            give(QKV, index, dot(turned[...], values).astype(low))
             grad[...] += dot(values, tile[...], (1, 1))
 
         return piece
@@ -1652,11 +1705,11 @@
     )
     pieces = [conv_piece(i) for i in range(len(groups))]
     gate(OUT, 1, width, STRIP)
-    weave(step(2), pieces[:7])
+    weave(step(2), pieces[:5])
     gate(QKV, qkv_strips, width, STRIP)
-    weave(step(3), pieces[7:14])
+    weave(step(3), pieces[5:11])
     gain_copy.wait()
-    weave(step(4), pieces[14:])
+    weave(step(4), pieces[11:])
     half = pack // 2
     here = pl.ds(pl.multiple_of(core_index * half, half), half)
     there = pl.ds(pl.multiple_of(other * half, half), half)
@@ -1699,8 +1752,9 @@
             slots = max(hop_slots(dims, order)[level] for order in orders)
             scratch.append(pltpu.VMEM((slots,) + block, low))
     tall_rows = pack + FINE
+    given = (grad_final, activated, middle_low, slope, unit_middle, attended, projected, unit_front, front_slope)
+    scratch += [pltpu.VMEM(one.shape, one.dtype) for one in given]
     scratch += [
-        pltpu.VMEM((pack, width), full),
         pltpu.VMEM((width, pack), low),
         pltpu.VMEM((pack, width), low),
         pltpu.VMEM((pack, 3 * width), low),
@@ -1725,6 +1779,7 @@
         pltpu.SemaphoreType.DMA((2, 2)),
         pltpu.SemaphoreType.DMA((4, 2)),
         pltpu.SemaphoreType.DMA((5,)),
+        pltpu.SemaphoreType.DMA((len(given),)),
     ]
     return pl.pallas_call(
         functools.partial(fused_backward_kernel, dims),
@@ -1737,14 +1792,13 @@
             shape((16, 2 * LANES), full),
             shape((2, pack // 2, width), full),
         ],
-        in_specs=[any_] * 6 + [vmem] * 12,
+        in_specs=[any_] * (5 + len(given)) + [vmem] * 4,
         out_specs=[vmem] * 7,
         scratch_shapes=scratch,
         compiler_params=pltpu.CompilerParams(
             collective_id=3, has_side_effects=True, vmem_limit_bytes=63 << 20
         ),
-    )(weight, wide, down, patches, probs, grad_final, gains, front_slope, unit_front, inverse_front,
-      projected, attended, unit_middle, inverse_middle, middle_low, slope, activated, gain_grads)
+    )(weight, wide, down, patches, probs, *given, gains, inverse_front, inverse_middle, gain_grads)
 
 
 GAIN_ROWS = 16
@@ -1824,7 +1878,7 @@
         )
         chunks = fused_chunks(conv_shard.shape[0], width, qkv_weight.shape[0], up_weight.shape[1], down_weight.shape[0])
         (weight, wide, down, patches, front_slope, unit_front, projected, probs, attended, unit_middle, middle_low,
-         outputs, gains, grad_final, inverse_front, inverse_middle, slope, activated, last_gain_grad) = fused_forward(
+         slope, activated, outputs, gains, grad_final, inverse_front, inverse_middle, last_gain_grad) = fused_forward(
             frames, cotangent, clip_lengths[:, 0], shards_in, chunks, dp
         )
         kept = (front_slope, grad_final, unit_front, inverse_front, projected, probs, attended, unit_middle,

time: 289 us -> 270 us (0.934)
  Pallas kernels: 263 us -> 245 us
    pallas_call x1, Pallas kernels: 136 us -> 125 us  [fused_backward(): pl.pallas_call(functools.partial(fused_backward_kernel, dims), out_shape=...]
    pallas_call x1, Pallas kernels: 127 us -> 119 us  [fused_forward(): pl.pallas_call(functools.partial(fused_forward_kernel, dims, chunks), out...]
where the time goes in v1:
time: 270 us; the launch traced here: 265 us
  Pallas kernels  245 us (91%)
  local copies, waits for them, and re-layouts  19.1 us (7%)
    pallas_call x1, Pallas kernels, fused_backward(): pl.pallas_call(functools.partial(fused_backward_kernel, dims), out_shape=...  125 us
    pallas_call x1, Pallas kernels, fused_forward(): pl.pallas_call(functools.partial(fused_forward_kernel, dims, chunks), out...  119 us
    unnamed x20, local copies, waits for them, and re-layouts  9.88 us

profile of v1, /device:TPU:0, one launch (start us, length us, event | category | flops | bytes accessed | tf_op | source)
XLA Modules:
  0.0 264.8 jit_solution(15814401083778313063)
XLA Ops:
  0.6 1.8 copy.23
  2.5 0.4 copy.24
  2.9 2.3 reshape.33.conv_shard
  5.2 119.4 %shard_map.186 = (bf16[16,384,768]{2,1,0:T(8,128)(2,1)}, bf16[768,6144]{1,0:T(8,128)(2,1)}, bf16[3072,768]{1,0:T(8,128)(2,1)}, bf16[16,272,384]{2,1,0:T(8,128)(2...) custom-call(s32[2,3]{1,0:T(2,128)} %bitcast.20, ...), custom_call_target="tpu_custom_call" | custom-call | tf_op jit(solution)/shard_map/pallas_call | solution.py:1223
  124.6 125.4 %shard_map.187 = (f32[384,768]{1,0:T(8,128)}, f32[48,2304]{1,0:T(8,128)}, f32[48,768]{1,0:T(8,128)}, f32[48,3072]{1,0:T(8,128)}, f32[192,768]{1,0:T(8,128)}, /*index=5*/f32[16,256]{1,0:T(8,128)}, f32[2,128,768]{2,1,0:T(8,128)}) custom-call(bf16[16,384,768]{2,1,0:T(8,128)(2,1)} %get-tuple-element.37.weight, bf16[768,6144]{1,0:T(8,128)(2,1)} %get-tuple-element.38.wide, ...), custom_call_target="tpu_custom_call" | custom-call | tf_op jit(solution)/shard_map/pallas_call | solution.py:1784
  250.0 1.3 slice_bitcast_fusion
  251.3 2.6 reshape.34
  254.0 2.6 copy.25
  256.6 0.0 copy-start.4
  256.6 0.0 copy-start
  256.6 0.0 copy-start.2
  256.6 3.3 %copy.26 = f32[128,48,48]{0,2,1:T(8,128)} copy(f32[128,48,48]{2,1,0:T(8,128)} %bitcast.18) | data formatting | bytes 2359296
  259.9 0.0 copy-done.4
  259.9 0.7 copy.33
  260.7 0.0 copy-done
  260.7 0.9 copy.34
  261.5 0.0 copy-done.3
  261.5 0.8 copy.35
  262.3 0.0 copy-done.5
  262.3 0.7 copy.36
  263.0 0.0 copy-done.2
  263.0 0.8 copy.37
  263.8 0.0 copy-done.1
  263.8 0.8 copy.38
  (3 shorter events, 0.0 us)
Async XLA Ops:
  256.6 3.4 %copy-start.4 = (bf16[2,128,768]{2,1,0:T(8,128)(2,1)S(1)}, bf16[2,128,768]{2,1,0:T(8,128)(2,1)}, u32[]{:S(2)}) copy-start(bf16[2,128,768]{2,1,0:T(8,128)(2,1)} %get-tuple-element.85) | copy-start | bytes 1179652
  256.6 4.1 %copy-start = (f32[2,128,768]{2,1,0:T(8,128)S(1)}, f32[2,128,768]{2,1,0:T(8,128)}, u32[]{:S(2)}) copy-start(f32[2,128,768]{2,1,0:T(8,128)} %get-tuple-element.86) | copy-start | bytes 2359300
  256.6 5.0 %copy-start.3 = (f32[48,2304]{1,0:T(8,128)S(1)}, f32[48,2304]{1,0:T(8,128)}, u32[]{:S(2)}) copy-start(f32[48,2304]{1,0:T(8,128)} %get-tuple-element.89) | copy-start | bytes 1327108
  256.6 5.7 %copy-start.5 = (f32[48,768]{1,0:T(8,128)S(1)}, f32[48,768]{1,0:T(8,128)}, u32[]{:S(2)}) copy-start(f32[48,768]{1,0:T(8,128)} %get-tuple-element.90) | copy-start | bytes 442372
  256.6 6.4 %copy-start.2 = (f32[48,3072]{1,0:T(8,128)S(1)}, f32[48,3072]{1,0:T(8,128)}, u32[]{:S(2)}) copy-start(f32[48,3072]{1,0:T(8,128)} %get-tuple-element.92) | copy-start | bytes 1769476
  259.9 3.9 %copy-start.1 = (f32[192,768]{1,0:T(8,128)S(1)}, f32[192,768]{1,0:T(8,128)}, u32[]{:S(2)}) copy-start(f32[192,768]{1,0:T(8,128)} %get-tuple-element.93) | copy-start | bytes 1769476

commit v2 on v1

--- a/solution.py
+++ b/solution.py
@@ -1258,7 +1258,7 @@
 
 STRIP = 384
 DOWN, UP, OUT, QKV, GAIN, CONV = range(6)
-CONV_PARTS = 4
+CONV_PARTS = 2
 SCATTER_ORDERS = (FIRST, FIRST, FIRST, FIRST, FIRST) + (FIRST,) * CONV_PARTS
 
 
@@ -1953,8 +1953,9 @@
 
     conv_sum = (
         conv_sum.reshape(COARSE, group_width, FINE, columns)
-        .transpose(0, 2, 1, 3)
-        .reshape(conv_weight.shape)
+        .transpose(1, 3, 0, 2)
+        .reshape(group_width, columns, KERNEL)
+        .transpose(2, 0, 1)
     )
     return (
         outputs,

time: 270 us -> 268 us (level)
  no operation moved by 1% of the time
where the time goes in v2:
time: 268 us; the launch traced here: 263 us
  Pallas kernels  243 us (91%)
  local copies, waits for them, and re-layouts  18.6 us (7%)
    pallas_call x1, Pallas kernels, fused_backward(): pl.pallas_call(functools.partial(fused_backward_kernel, dims), out_shape=...  124 us
    pallas_call x1, Pallas kernels, fused_forward(): pl.pallas_call(functools.partial(fused_forward_kernel, dims, chunks), out...  119 us
    unnamed x20, local copies, waits for them, and re-layouts  9.85 us

profile of v2, /device:TPU:0, one launch (start us, length us, event | category | flops | bytes accessed | tf_op | source)
XLA Modules:
  0.0 263.1 jit_solution(4342132052557195213)
XLA Ops:
  0.6 1.8 copy.23
  2.5 0.4 copy.24
  2.9 2.3 reshape.33.conv_shard
  5.2 119.3 %shard_map.186 = (bf16[16,384,768]{2,1,0:T(8,128)(2,1)}, bf16[768,6144]{1,0:T(8,128)(2,1)}, bf16[3072,768]{1,0:T(8,128)(2,1)}, bf16[16,272,384]{2,1,0:T(8,128)(2...) custom-call(s32[2,3]{1,0:T(2,128)} %bitcast.22, ...), custom_call_target="tpu_custom_call" | custom-call | tf_op jit(solution)/shard_map/pallas_call | solution.py:1223
  124.5 124.1 %shard_map.187 = (f32[384,768]{1,0:T(8,128)}, f32[48,2304]{1,0:T(8,128)}, f32[48,768]{1,0:T(8,128)}, f32[48,3072]{1,0:T(8,128)}, f32[192,768]{1,0:T(8,128)}, /*index=5*/f32[16,256]{1,0:T(8,128)}, f32[2,128,768]{2,1,0:T(8,128)}) custom-call(bf16[16,384,768]{2,1,0:T(8,128)(2,1)} %get-tuple-element.37.weight, bf16[768,6144]{1,0:T(8,128)(2,1)} %get-tuple-element.38.wide, ...), custom_call_target="tpu_custom_call" | custom-call | tf_op jit(solution)/shard_map/pallas_call | solution.py:1784
  248.6 1.3 slice_bitcast_fusion
  249.9 2.6 %reshape.34 = f32[8,48,16,48]{3,2,1,0:T(8,128)S(1)} reshape(f32[384,768]{1,0:T(8,128)} %get-tuple-element.56) | data formatting | bytes 2359296 | tf_op jit(solution)/shard_map/reshape | solution.py:1955
  252.6 2.1 copy.25
  254.7 0.0 copy-start.4
  254.7 0.0 copy-start
  254.7 0.0 copy-start.2
  254.7 3.3 %copy.26 = f32[128,48,48]{0,2,1:T(8,128)} copy(f32[128,48,48]{2,0,1:T(8,128)} %bitcast.20) | data formatting | bytes 2359296
  258.0 0.0 copy-done.4
  258.0 0.7 copy.33
  258.7 0.0 copy-done
  258.7 0.9 copy.34
  259.6 0.0 copy-done.3
  259.6 0.8 copy.35
  260.4 0.0 copy-done.5
  260.4 0.7 copy.36
  261.0 0.0 copy-done.2
  261.0 0.8 copy.37
  261.9 0.0 copy-done.1
  261.9 0.8 copy.38
  (3 shorter events, 0.0 us)
Async XLA Ops:
  254.7 3.3 %copy-start.4 = (bf16[2,128,768]{2,1,0:T(8,128)(2,1)S(1)}, bf16[2,128,768]{2,1,0:T(8,128)(2,1)}, u32[]{:S(2)}) copy-start(bf16[2,128,768]{2,1,0:T(8,128)(2,1)} %get-tuple-element.85) | copy-start | bytes 1179652
  254.7 4.1 %copy-start = (f32[2,128,768]{2,1,0:T(8,128)S(1)}, f32[2,128,768]{2,1,0:T(8,128)}, u32[]{:S(2)}) copy-start(f32[2,128,768]{2,1,0:T(8,128)} %get-tuple-element.86) | copy-start | bytes 2359300
  254.7 5.0 %copy-start.3 = (f32[48,2304]{1,0:T(8,128)S(1)}, f32[48,2304]{1,0:T(8,128)}, u32[]{:S(2)}) copy-start(f32[48,2304]{1,0:T(8,128)} %get-tuple-element.89) | copy-start | bytes 1327108
  254.7 5.7 %copy-start.5 = (f32[48,768]{1,0:T(8,128)S(1)}, f32[48,768]{1,0:T(8,128)}, u32[]{:S(2)}) copy-start(f32[48,768]{1,0:T(8,128)} %get-tuple-element.90) | copy-start | bytes 442372
  254.7 6.4 %copy-start.2 = (f32[48,3072]{1,0:T(8,128)S(1)}, f32[48,3072]{1,0:T(8,128)}, u32[]{:S(2)}) copy-start(f32[48,3072]{1,0:T(8,128)} %get-tuple-element.92) | copy-start | bytes 1769476
  258.0 3.9 %copy-start.1 = (f32[192,768]{1,0:T(8,128)S(1)}, f32[192,768]{1,0:T(8,128)}, u32[]{:S(2)}) copy-start(f32[192,768]{1,0:T(8,128)} %get-tuple-element.93) | copy-start | bytes 1769476
